TPU v7x, 256 devices: a whole 4x4x8 slice. The times are simulated.
256 devices in a mesh: particle: 32 (over z, x_lo, core), space: 8 (over x_hi, y).
Axes of the slice: x: 4 (x_hi: 2, x_lo: 2; x = x_hi * 2 + x_lo), y: 4, z: 8, core: 2. Of those that a mesh axis runs over, the one named last changes fastest.
Arguments:
- coeffs: float32 [32, 4096], P('particle'), may hold values from -1.6 to 1.6
- modes: int32 [4096], replicated, may hold values from 0 to 4095, each once
- basis_x: float32 [128, 16], replicated, may hold values from -1.5 to 1.5
- basis_y: float32 [128, 16], replicated, may hold values from -1.5 to 1.5
- basis_z: float32 [128, 16], replicated, may hold values from -1.5 to 1.5
- pressure: float32 [32, 128, 128, 128], P('particle', 'space'), may hold values from -6 to 6
- initial_adjoint: float32 [32, 128, 128, 128], P('particle', 'space'), may hold values from -3 to 3
- sensors: int32 [1024], replicated, may hold values from 0 to 2097151, as said below
- observed: float32 [1024], replicated, may hold values from -6 to 6
- precision: float32 [1024], replicated, may hold values from 0.5 to 2
Outputs:
- new_coeffs: float32 [32, 4096], P('particle', 'space')
- adjoint: float32 [32, 128, 128, 128], P('particle', 'space')
Inputs may be any that keep to these rules, and one draw needn't show every extreme that they name: The sensors are distinct and increasing; sensor s lies in the run of 2048 consecutive flat cells starting at s times that run.
All inputs are finite; a program needn't handle non-finite values.
Results may differ from a plain program's by a relative error of at most 0.0017.
Values sent between devices are 32-bit elements; how exact they have to be, the bound alone decides.
A program may use at most 64 MiB of HBM per device.

v0:
```python
import jax
import jax.numpy as jnp
from jax import lax
from jax.sharding import PartitionSpec as P

ITERS = 2


HIGH = lax.Precision.HIGHEST
STEP = 0.5
MID = slice(1, -1)
SHIFTS = (
    (slice(2, None), MID, MID),
    (slice(None, -2), MID, MID),
    (MID, slice(2, None), MID),
    (MID, slice(None, -2), MID),
    (MID, MID, slice(2, None)),
    (MID, MID, slice(None, -2)),
)


def padded(value, sides, width):
    for axis, dim in sides:
        peers, length = (lax.axis_size(axis), value.shape[dim])
        up = [(i, (i + 1) % peers) for i in range(peers - 1)]
        down = [(j, i) for i, j in up]
        last = lax.slice_in_dim(value, length - width, length, axis=dim)
        first = lax.slice_in_dim(value, 0, width, axis=dim)
        before = lax.ppermute(last, axis, up)
        after = lax.ppermute(first, axis, down)
        value = jnp.concatenate([before, value, after], axis=dim)
    return value


def log_field(xi, modes, x_rows, basis_y, basis_z):
    msize = basis_y.shape[1]
    flat = jnp.zeros((msize * msize * msize,), jnp.float32).at[modes].set(xi)
    tensor = flat.reshape(msize, msize, msize)
    first = jnp.einsum("ijl,zl->ijz", tensor, basis_z, precision=HIGH)
    second = jnp.einsum("ijz,yj->iyz", first, basis_y, precision=HIGH)
    return jnp.einsum("iyz,xi->xyz", second, x_rows, precision=HIGH)


def apply_op(v_pad, kap_pad):
    center = v_pad[MID, MID, MID]
    kap_mid = kap_pad[MID, MID, MID]
    total = jnp.zeros_like(center)
    for shift in SHIFTS:
        total = total + 0.5 * (kap_mid + kap_pad[shift]) * (center - v_pad[shift])
    return total


def project(cellgrad, x_rows, basis_y, basis_z):
    first = jnp.einsum("xyz,zl->xyl", cellgrad, basis_z, precision=HIGH)
    second = jnp.einsum("xyl,yj->xjl", first, basis_y, precision=HIGH)
    return jnp.einsum("xjl,xi->ijl", second, x_rows, precision=HIGH).reshape(-1)


def pad_sides(field):
    return jnp.pad(field, ((0, 0), (1, 1), (1, 1)))


def shards(
    coeffs,
    modes,
    basis_x,
    basis_y,
    basis_z,
    pressure,
    initial_adjoint,
    sensors,
    observed,
    precision,
):
    own = coeffs[0]
    field_p = pressure[0]
    warm_start = initial_adjoint[0]
    cells_x, cells_y, cells_z = field_p.shape
    spaces = lax.axis_size("space")
    start = lax.axis_index("space") * cells_x
    total_x = cells_x * spaces
    rows = jnp.clip(start - 1 + jnp.arange(cells_x + 2), 0, total_x - 1)
    kap_rows = jnp.exp(log_field(own, modes, basis_x[rows], basis_y, basis_z))
    kap_pad = jnp.pad(kap_rows, ((0, 0), (1, 1), (1, 1)), mode="edge")
    kappa = kap_rows[1:-1]
    slab = cells_x * cells_y * cells_z
    offset = sensors - start * cells_y * cells_z
    inside = (offset >= 0) & (offset < slab)
    safe = jnp.clip(offset, 0, slab - 1)
    picks = field_p.reshape(-1)[safe]
    weighted = (picks - observed) * precision
    rhs = (
        jnp.zeros((slab,), jnp.float32)
        .at[safe]
        .add(jnp.where(inside, weighted, 0.0))
        .reshape(cells_x, cells_y, cells_z)
    )
    start_rim = padded(warm_start, (("space", 0),), 1)
    solved = warm_start
    resid = rhs - apply_op(pad_sides(start_rim), kap_pad)
    direction = resid
    norm_now = lax.psum(jnp.sum(resid * resid), "space")
    for step in range(ITERS):
        extended = padded(direction, (("space", 0),), 1)
        image = apply_op(pad_sides(extended), kap_pad)
        alpha = norm_now / lax.psum(jnp.sum(direction * image), "space")
        solved = solved + alpha * direction
        resid = resid - alpha * image
        if step + 1 < ITERS:
            norm_next = lax.psum(jnp.sum(resid * resid), "space")
            direction = resid + norm_next / norm_now * direction
            norm_now = norm_next
    states = padded(jnp.stack([solved, field_p]), (("space", 1),), 1)
    adjoint_rim = states[0]
    pressure_rim = states[1]
    lam_pad = pad_sides(adjoint_rim)
    pre_pad = pad_sides(pressure_rim)
    global_x = (start + jnp.arange(cells_x))[:, None, None]
    local_y = jnp.arange(cells_y)[None, :, None]
    local_z = jnp.arange(cells_z)[None, None, :]
    edges = (
        global_x == total_x - 1,
        global_x == 0,
        local_y == cells_y - 1,
        local_y == 0,
        local_z == cells_z - 1,
        local_z == 0,
    )
    total = jnp.zeros_like(rhs)
    for shift, edge in zip(SHIFTS, edges):
        factor = 0.5 + 0.5 * edge.astype(jnp.float32)
        total = total + factor * (solved - lam_pad[shift]) * (field_p - pre_pad[shift])
    cellgrad = kappa * total
    local_rows = lax.dynamic_slice_in_dim(basis_x, start, cells_x, 0)
    partial_value = project(cellgrad, local_rows, basis_y, basis_z)[modes]
    coef_count = own.shape[0]
    share = coef_count // spaces
    summed = lax.psum(partial_value, "space")
    grad = -own - summed
    all_x, all_g = (
        lax.all_gather(coeffs, "particle", axis=0, tiled=True),
        lax.all_gather(grad[None], "particle", axis=0, tiled=True),
    )
    count = all_x.shape[0]
    dist_row = jnp.sum((all_x - own) ** 2, axis=1)
    centered = all_x - jnp.mean(all_x, axis=0)
    width = 2.0 * jnp.sum(centered * centered) / (count - 1)
    kern = jnp.exp(-dist_row / width)
    drive = jnp.dot(kern, all_g, precision=HIGH)
    repel = own * jnp.sum(kern) - jnp.dot(kern, all_x, precision=HIGH)
    updated = own + STEP * (drive + 2.0 / width * repel) / count
    new_share = lax.dynamic_slice_in_dim(updated, lax.axis_index("space") * share, share, 0)[None]
    return (new_share, solved[None])


def solution(mesh):
    in_specs = (
        P("particle", None),
        P(),
        P(),
        P(),
        P(),
        P("particle", "space", None, None),
        P("particle", "space", None, None),
        P(),
        P(),
        P(),
    )
    out_specs = (P("particle", "space"), P("particle", "space", None, None))
    return jax.shard_map(shards, mesh=mesh, in_specs=in_specs, out_specs=out_specs, check_vma=False)
```

profile of v0, /device:TPU:1, one launch (start us, length us, event | category | flops | bytes accessed | tf_op | source)
XLA Modules:
  0.0 329.1 jit_solution(16400094809866302995)
XLA Ops:
  0.6 0.9 fusion.163
  1.5 1.3 collective-permute-start
  2.8 4.7 %collective-permute-start.1 = (f32[1,128,128]{2,0,1:T(1,128)S(1)}, f32[1,128,128]{2,0,1:T(1,128)S(1)}, u32[]{:S(2)}, u32[]{:S(2)}) collective-permute-start(f32[1,128,128]{2,0,1:T(1,128)S(1)} %bitcast.121), channel_id=1, source_target_pairs={{0,1},{1,2},{2,3},{3,4},{4,5},{5,6},{6,7},{8,9},{9,10},{10,11},{11... | collective-permute-start | bytes 196616 | tf_op jit(solution)/shard_map/ppermute | solution.py:29
  7.5 0.8 copy.26
  8.3 0.7 broadcast_clamp_fusion
  9.1 15.7 %scatter_custom_fusion = f32[4096]{0:T(1024)S(1)} fusion(s32[4096]{0:T(1024)S(1)} %get-tuple-element.39, f32[4096]{0:T(1024)} %bitcast.116, f32[]{:T(128)} %constant.16.clone.1), kind=kCustom, calls=%fused_computation.203 | custom fusion | bytes 16896 | tf_op jit(solution)/shard_map/scatter | solution.py:37
  24.9 0.9 fusion.132
  25.8 1.8 convolution_bitcast_fusion
  27.6 0.5 copy.28
  28.2 0.6 gather_fusion
  28.7 1.4 convolution_exponential_fusion
  30.2 0.1 pad_maximum_fusion.1
  30.3 2.2 fusion.159
  32.5 39.8 %all-gather.1 = f32[32,1,4096]{2,1,0:T(1,128)S(1)} all-gather(f32[1,1,4096]{2,1,0:T(1,128)S(1)} %bitcast.117), channel_id=1, replica_groups=mesh['particle'=32,'space'=8] {'particle'}, dimensions={0}, use_global_device_ids=true | all-gather | bytes 540672 | tf_op jit(solution)/shard_map/all_gather | solution.py:141
  72.3 0.4 reduce_sum.73
  72.7 6.2 %gather_fusion.1 = f32[1024]{0:T(1024)S(1)} fusion(f32[262144]{0:T(1024)S(1)} %bitcast.108, s32[1024]{0:T(1024)S(1)} %get-tuple-element.22), kind=kCustom, calls=%fused_computation.1 | custom fusion | bytes 12288 | tf_op jit(solution)/shard_map/gather | solution.py:90
  78.9 1.8 copy.54
  80.7 8.5 %scatter_custom_fusion.1 = f32[262144]{0:T(1024)} fusion(s32[1024]{0:T(1024)S(1)} %get-tuple-element.23, f32[1024]{0:T(1024)S(1)} %multiply_select_fusion, f32[]{:T(128)} %constant.16.clone.1), kind=kCustom, calls=%fused_computation.185 | custom fusion | flops 1024 | bytes 1048580 | tf_op jit(solution)/shard_map/scatter-add | solution.py:95
  89.2 1.4 select_maximum_fusion.4
  90.7 0.4 copy-done.17
  91.1 0.3 copy-done.18
  91.4 8.2 %fusion.89 = (f32[16,128,128]{2,0,1:T(8,128)S(1)}, f32[16,128,128]{2,0,1:T(8,128)}, f32[16,128,128]{2,0,1:T(8,128)}, f32[16,128,128]{2,0,1:T(8,128)}, f32[16,128,128]{2,0,1:T(8,128)}) fusion(f32[16,128,128]{2,0,1:T(8,128)} %bitcast.114, f32[18,130,130]{2,0,1:T(8,128)S(1)} %select_maximum_fusion.4, f32[1,128,128]{2,0,1:T(1,128)S(1)} %collective-permute-done.1, ...), kind=kLoop, calls=%fused_computation.126 | loop fusion | flops 10485760 | bytes 19603456 | tf_op jit(solution)/shard_map/sub | solution.py:100
  99.6 0.1 fusion.162
  99.7 1.3 collective-permute-start.2
  101.0 4.0 %collective-permute-start.3 = (f32[1,128,128]{2,0,1:T(1,128)S(1)}, f32[1,128,128]{2,0,1:T(1,128)S(1)}, u32[]{:S(2)}, u32[]{:S(2)}) collective-permute-start(f32[1,128,128]{2,0,1:T(1,128)S(1)} %get-tuple-element.34), channel_id=1, source_target_pairs={{0,1},{1,2},{2,3},{3,4},{4,5},{5,6},{6,7},{8,9},{9,10},{10,11},{11... | collective-permute-start | bytes 196616 | tf_op jit(solution)/shard_map/ppermute | solution.py:29
  105.0 1.0 fusion.118
  106.8 1.4 select_maximum_fusion.2
  108.2 0.3 copy-done.10
  108.6 0.3 copy-done.12
  108.9 3.5 %multiply_reduce_fusion.1 = (f32[]{:T(128)}, f32[]{:T(128)}, f32[16,128,128]{2,0,1:T(8,128)}) fusion(f32[16,128,128]{2,0,1:T(8,128)S(1)} %get-tuple-element.17, f32[16,128,128]{2,0,1:T(8,128)S(1)} %copy-done.12, f32[18,130,130]{2,0,1:T(8,128)S(1)} %select_maximum_fusion.2, f32[16,128,128]{2,0,1:T(8,128)S(1)} %copy-done.10, ...), kind=kLoop, calls=%fused_computation.169 | loop fusion | flops 7077886 | bytes 13762568 | tf_op jit(solution)/shard_map/reduce_sum | solution.py:106
  112.4 22.1 %all-reduce.5 = (f32[]{:T(128)}, f32[]{:T(128)}) all-reduce(f32[]{:T(128)} %get-tuple-element.9, f32[]{:T(128)} %get-tuple-element.8), channel_id=1, replica_groups=mesh['particle'=32,'space'=8] {'space'}, use_global_device_ids=true, to_apply=%region_6.7 | all-reduce | flops 2 | bytes 16 | tf_op jit(solution)/shard_map/psum | solution.py:102
  135.8 2.1 multiply_reduce_fusion
  137.9 0.6 fusion.153
  138.5 20.1 %psum.37 = f32[]{:T(128)} all-reduce(f32[]{:T(128)} %multiply_reduce_fusion), channel_id=1, replica_groups=mesh['particle'=32,'space'=8] {'space'}, use_global_device_ids=true, to_apply=%region_10.11 | all-reduce | flops 1 | bytes 8 | tf_op jit(solution)/shard_map/psum | solution.py:110
  159.9 1.5 multiply_add_fusion.1
  161.4 0.1 fusion.161
  161.5 1.6 collective-permute-start.4
  163.1 4.0 %collective-permute-start.5 = (f32[1,128,128]{2,0,1:T(1,128)S(1)}, f32[1,128,128]{2,0,1:T(1,128)S(1)}, u32[]{:S(2)}, u32[]{:S(2)}) collective-permute-start(f32[1,128,128]{2,0,1:T(1,128)S(1)} %get-tuple-element.32), channel_id=1, source_target_pairs={{0,1},{1,2},{2,3},{3,4},{4,5},{5,6},{6,7},{8,9},{9,10},{10,11},{11... | collective-permute-start | bytes 196616 | tf_op jit(solution)/shard_map/ppermute | solution.py:29
  167.1 0.6 fusion.113
  167.7 0.7 collective-permute-done.5
  168.4 1.4 select_maximum_fusion
  169.9 2.8 fusion.62
  172.6 1.6 copy.31
  174.2 21.0 %psum.38 = f32[]{:T(128)} all-reduce(f32[]{:T(128)} %fusion.62), channel_id=1, replica_groups=mesh['particle'=32,'space'=8] {'space'}, use_global_device_ids=true, to_apply=%region_12.13 | all-reduce | flops 1 | bytes 8 | tf_op jit(solution)/shard_map/psum | solution.py:106
  196.5 2.3 multiply_add_fusion
  198.9 1.0 copy-done.3
  199.9 0.2 pad_maximum_fusion.22
  200.1 1.3 collective-permute-start.6
  201.4 4.0 %collective-permute-start.7 = (f32[2,1,128,128]{3,1,2,0:T(1,128)S(1)}, f32[2,1,128,128]{3,1,2,0:T(1,128)S(1)}, u32[]{:S(2)}, u32[]{:S(2)}) collective-permute-start(f32[2,1,128,128]{3,1,2,0:T(1,128)S(1)} %get-tuple-element.26), channel_id=1, source_target_pairs={{0,1},{1,2},{2,3},{3,4},{4,5},{5,6},{6,7},{8,9},{9,10},{10,11},{11... | collective-permute-start | bytes 393224 | tf_op jit(solution)/shard_map/ppermute | solution.py:29
  205.5 2.5 copy.36
  208.0 1.8 pad_maximum_fusion
  209.8 0.2 slice_bitcast_fusion
  210.0 1.0 copy-done.4
  211.0 3.1 fusion.11
  214.1 1.8 convolution_bitcast_fusion.1
  215.9 0.1 copy.34
  216.1 0.3 fusion.134
  216.5 0.1 reshape.97
  216.6 23.0 %gather_fusion.2 = f32[4096]{0:T(1024)S(1)} fusion(f32[4096]{0:T(1024)S(1)} %reshape.97, s32[4096]{0:T(1024)S(1)} %get-tuple-element.38), kind=kCustom, calls=%fused_computation.2 | custom fusion | bytes 49152 | tf_op jit(solution)/shard_map/gather | solution.py:135
  239.6 34.3 %psum.39 = f32[4096]{0:T(1024)S(1)} all-reduce(f32[4096]{0:T(1024)S(1)} %gather_fusion.2), channel_id=1, replica_groups=mesh['particle'=32,'space'=8] {'space'}, use_global_device_ids=true, to_apply=%region_13.14 | all-reduce | flops 4096 | bytes 32768 | tf_op jit(solution)/shard_map/psum | solution.py:138
  274.0 53.4 %all-gather = f32[131072]{0:T(1024)S(1)} all-gather(f32[4096]{0:T(1024)S(1)} %negate_subtract_fusion), channel_id=2, replica_groups=mesh['particle'=32,'space'=8] {'particle'}, dimensions={0}, use_global_device_ids=true | all-gather | bytes 540672 | tf_op jit(solution)/shard_map/all_gather | solution.py:142
  327.4 0.1 reshape.138
  327.5 0.4 fusion.148
  327.9 1.3 fusion.140
  (62 shorter events, 0.4 us)
Async XLA Ops:
  0.6 25.2 %copy-start = (f32[128,16]{0,1:T(8,128)S(1)}, f32[128,16]{0,1:T(8,128)}, u32[]{:S(2)}) copy-start(f32[128,16]{0,1:T(8,128)} %param.13) | copy-start | bytes 24580
  1.5 87.7 %collective-permute-start = (f32[1,128,128]{2,0,1:T(1,128)S(1)}, f32[1,128,128]{2,0,1:T(1,128)S(1)}, u32[]{:S(2)}, u32[]{:S(2)}) collective-permute-start(f32[1,128,128]{2,0,1:T(1,128)S(1)} %bitcast.122), channel_id=1, source_target_pairs={{1,0},{2,1},{3,2},{4,3},{5,4},{6,5},{7,6},{9,8},{10,9},{11,10},{12... | collective-permute-start | bytes 196616 | tf_op jit(solution)/shard_map/ppermute | solution.py:30
  2.8 86.4 %collective-permute-start.1 = (f32[1,128,128]{2,0,1:T(1,128)S(1)}, f32[1,128,128]{2,0,1:T(1,128)S(1)}, u32[]{:S(2)}, u32[]{:S(2)}) collective-permute-start(f32[1,128,128]{2,0,1:T(1,128)S(1)} %bitcast.121), channel_id=1, source_target_pairs={{0,1},{1,2},{2,3},{3,4},{4,5},{5,6},{6,7},{8,9},{9,10},{10,11},{11... | collective-permute-start | bytes 196616 | tf_op jit(solution)/shard_map/ppermute | solution.py:29
  30.3 2.2 copy-start.19
  30.3 42.3 %copy-start.21 = (s32[1024]{0:T(1024)S(1)}, s32[1024]{0:T(1024)}, u32[]{:S(2)}) copy-start(s32[1024]{0:T(1024)} %param.17) | copy-start | bytes 12292
  30.3 42.4 %copy-start.1 = (f32[1,16,128,128]{3,2,1,0:T(8,128)S(1)}, f32[1,16,128,128]{3,2,1,0:T(8,128)}, u32[]{:S(2)}) copy-start(f32[1,16,128,128]{3,2,1,0:T(8,128)} %param.15) | copy-start | bytes 3145732
  32.5 46.4 %copy-start.23 = (f32[1024]{0:T(1024)S(1)}, f32[1024]{0:T(1024)}, u32[]{:S(2)}) copy-start(f32[1024]{0:T(1024)} %param.19) | copy-start | bytes 12292
  32.5 46.4 %copy-start.24 = (f32[1024]{0:T(1024)S(1)}, f32[1024]{0:T(1024)}, u32[]{:S(2)}) copy-start(f32[1024]{0:T(1024)} %param.18) | copy-start | bytes 12292
  80.7 9.9 %copy-start.5 = (f32[1,16,128,128]{3,1,2,0:T(8,128)}, f32[1,16,128,128]{3,1,2,0:T(8,128)S(1)}, u32[]{:S(2)}) copy-start(f32[1,16,128,128]{3,1,2,0:T(8,128)S(1)} %copy.54) | copy-start | bytes 3145732
  89.2 1.5 copy-start.16
  89.2 1.9 copy-start.17
  89.2 2.2 copy-start.18
  99.7 7.0 %collective-permute-start.2 = (f32[1,128,128]{2,0,1:T(1,128)S(1)}, f32[1,128,128]{2,0,1:T(1,128)S(1)}, u32[]{:S(2)}, u32[]{:S(2)}) collective-permute-start(f32[1,128,128]{2,0,1:T(1,128)S(1)} %get-tuple-element.35), channel_id=1, source_target_pairs={{1,0},{2,1},{3,2},{4,3},{5,4},{6,5},{7,6},{9,8},{10,9},{11,10},{12... | collective-permute-start | bytes 196616 | tf_op jit(solution)/shard_map/ppermute | solution.py:30
  101.0 5.7 %collective-permute-start.3 = (f32[1,128,128]{2,0,1:T(1,128)S(1)}, f32[1,128,128]{2,0,1:T(1,128)S(1)}, u32[]{:S(2)}, u32[]{:S(2)}) collective-permute-start(f32[1,128,128]{2,0,1:T(1,128)S(1)} %get-tuple-element.34), channel_id=1, source_target_pairs={{0,1},{1,2},{2,3},{3,4},{4,5},{5,6},{6,7},{8,9},{9,10},{10,11},{11... | collective-permute-start | bytes 196616 | tf_op jit(solution)/shard_map/ppermute | solution.py:29
  106.7 1.5 copy-start.6
  106.7 1.5 copy-start.8
  106.7 1.8 copy-start.10
  106.7 2.1 copy-start.12
  161.4 8.4 %copy-start.7 = (f32[16,128,128]{2,0,1:T(8,128)S(1)}, f32[16,128,128]{2,0,1:T(8,128)}, u32[]{:S(2)}) copy-start(f32[16,128,128]{2,0,1:T(8,128)} %get-tuple-element.18) | copy-start | bytes 3145732
  161.4 8.4 %copy-start.9 = (f32[16,128,128]{2,0,1:T(8,128)S(1)}, f32[16,128,128]{2,0,1:T(8,128)}, u32[]{:S(2)}) copy-start(f32[16,128,128]{2,0,1:T(8,128)} %get-tuple-element.19) | copy-start | bytes 3145732
  161.4 8.4 %copy-start.11 = (f32[16,128,128]{2,0,1:T(8,128)S(1)}, f32[16,128,128]{2,0,1:T(8,128)}, u32[]{:S(2)}) copy-start(f32[16,128,128]{2,0,1:T(8,128)} %get-tuple-element.20) | copy-start | bytes 3145732
  161.4 8.4 %copy-start.13 = (f32[16,128,128]{2,0,1:T(8,128)S(1)}, f32[16,128,128]{2,0,1:T(8,128)}, u32[]{:S(2)}) copy-start(f32[16,128,128]{2,0,1:T(8,128)} %get-tuple-element.21) | copy-start | bytes 3145732
  161.5 6.2 %collective-permute-start.4 = (f32[1,128,128]{2,0,1:T(1,128)S(1)}, f32[1,128,128]{2,0,1:T(1,128)S(1)}, u32[]{:S(2)}, u32[]{:S(2)}) collective-permute-start(f32[1,128,128]{2,0,1:T(1,128)S(1)} %get-tuple-element.33), channel_id=1, source_target_pairs={{1,0},{2,1},{3,2},{4,3},{5,4},{6,5},{7,6},{9,8},{10,9},{11,10},{12... | collective-permute-start | bytes 196616 | tf_op jit(solution)/shard_map/ppermute | solution.py:30
  163.1 5.3 %collective-permute-start.5 = (f32[1,128,128]{2,0,1:T(1,128)S(1)}, f32[1,128,128]{2,0,1:T(1,128)S(1)}, u32[]{:S(2)}, u32[]{:S(2)}) collective-permute-start(f32[1,128,128]{2,0,1:T(1,128)S(1)} %get-tuple-element.32), channel_id=1, source_target_pairs={{0,1},{1,2},{2,3},{3,4},{4,5},{5,6},{6,7},{8,9},{9,10},{10,11},{11... | collective-permute-start | bytes 196616 | tf_op jit(solution)/shard_map/ppermute | solution.py:29
  169.8 2.8 copy-start.2
  196.5 3.4 %copy-start.14 = (f32[1,16,128,128]{3,1,2,0:T(8,128)S(1)}, f32[1,16,128,128]{3,1,2,0:T(8,128)}, u32[]{:S(2)}) copy-start(f32[1,16,128,128]{3,1,2,0:T(8,128)} %copy.31) | copy-start | bytes 3145732
  198.9 1.0 copy-start.3
  198.9 9.1 %copy-start.15 = (f32[1,16,128,128]{3,1,2,0:T(8,128)S(1)}, f32[1,16,128,128]{3,1,2,0:T(8,128)}, u32[]{:S(2)}) copy-start(f32[1,16,128,128]{3,1,2,0:T(8,128)} %copy.31) | copy-start | bytes 3145732
  200.1 7.9 %collective-permute-start.6 = (f32[2,1,128,128]{3,1,2,0:T(1,128)S(1)}, f32[2,1,128,128]{3,1,2,0:T(1,128)S(1)}, u32[]{:S(2)}, u32[]{:S(2)}) collective-permute-start(f32[2,1,128,128]{3,1,2,0:T(1,128)S(1)} %get-tuple-element.27), channel_id=1, source_target_pairs={{1,0},{2,1},{3,2},{4,3},{5,4},{6,5},{7,6},{9,8},{10,9},{11,10},{12... | collective-permute-start | bytes 393224 | tf_op jit(solution)/shard_map/ppermute | solution.py:30
  201.4 6.6 %collective-permute-start.7 = (f32[2,1,128,128]{3,1,2,0:T(1,128)S(1)}, f32[2,1,128,128]{3,1,2,0:T(1,128)S(1)}, u32[]{:S(2)}, u32[]{:S(2)}) collective-permute-start(f32[2,1,128,128]{3,1,2,0:T(1,128)S(1)} %get-tuple-element.26), channel_id=1, source_target_pairs={{0,1},{1,2},{2,3},{3,4},{4,5},{5,6},{6,7},{8,9},{9,10},{10,11},{11... | collective-permute-start | bytes 393224 | tf_op jit(solution)/shard_map/ppermute | solution.py:29
  209.8 1.2 copy-start.4
  209.8 1.2 copy-start.22
  211.0 5.0 %copy-start.20 = (f32[128,16]{0,1:T(8,128)S(1)}, f32[128,16]{0,1:T(8,128)}, u32[]{:S(2)}) copy-start(f32[128,16]{0,1:T(8,128)} %param.12) | copy-start | bytes 24580
where the time goes:
time: 331 us; the launch traced here: 329 us
  blocking collectives  191 us (58%)
  local copies, waits for them, and re-layouts  60.1 us (18%)
  other arithmetic  39.3 us (12%)
  starting transfers between devices  22.1 us (7%)
  matrix products  10.4 us (3%)
  between operations  5.77 us (2%)
    all_gather x1, blocking collectives, shards(): lax.all_gather(grad[None], 'particle', axis=0, tiled=True)  53.4 us
    all_gather x1, blocking collectives, shards(): lax.all_gather(coeffs, 'particle', axis=0, tiled=True)  39.8 us
    psum x1, blocking collectives, shards(): summed = lax.psum(partial_value, 'space')  34.3 us
    gather x1, local copies, waits for them, and re-layouts, shards(): partial_value = project(cellgrad, local_rows, basis_y, basis_z)[modes]  23 us
    psum x1, blocking collectives, shards(): norm_now = lax.psum(jnp.sum(resid * resid), 'space')  22.1 us
    psum x1, blocking collectives, shards(): alpha = norm_now / lax.psum(jnp.sum(direction * image), 'space')  21 us
    psum x1, blocking collectives, shards(): norm_next = lax.psum(jnp.sum(resid * resid), 'space')  20.1 us
    ppermute x4, starting transfers between devices, padded(): before = lax.ppermute(last, axis, up)  16.6 us
  transfers between devices with their start and end apart: 8, of which 1 were waited for; matrix products, arithmetic and copies ran while one was open for 14% of the time, Pallas kernels for 0%

commit v1 on v0

v1 whole, which is shorter than its diff:
```python
import jax
import jax.numpy as jnp
from jax import lax
from jax.experimental import pallas as pl
from jax.experimental.pallas import tpu as pltpu
from jax.sharding import PartitionSpec as P

F32 = jnp.float32
BF16 = jnp.bfloat16
NP = 32
NS = 8
LX = 16
NX = 128
NG = 128
M = 16
K = M * M * M
SH = K // NS
HALO = 3
STEP = 0.5
NN = (((1,), (1,)), ((), ()))


def pieces(value, count):
    out = []
    rest = value
    for _ in range(count):
        part = rest.astype(BF16)
        out.append(part)
        rest = rest - part.astype(F32)
    return out


def mm(a, b):
    return jnp.dot(a, b, preferred_element_type=F32)


def mm_nt(a, b):
    return lax.dot_general(a, b, NN, preferred_element_type=F32)


def fold(value):
    return jnp.sum(value.reshape(NG // 8, 8, NG), axis=0)


def kernel(
    c_hbm, modes_ref, bx_ref, by_ref, bz_ref, p_hbm, x_hbm, sens_ref, obs_ref, prec_ref,
    new_ref, adj_hbm,
    xe, pe, kp, kx, ky, kz, kb, u0, u1, xo, rsum, hot, lhot, lcs, bylhs, fbuf, pbuf, qbuf,
    cs, wk, pk, rp, gs, mom,
    in_sem, out_sem, halo_send, halo_recv, c_own, c_send, c_recv, m_send, m_recv, r_send, r_recv, g_send, g_recv,
):
    n = lax.axis_index("particle")
    s = lax.axis_index("space")
    first = s == 0
    last = s == NS - 1

    def peer_p(r):
        return {"particle": lax.rem(n + r, NP)}

    def peer_s(r):
        return {"space": lax.rem(s + r, NS)}

    barrier = pltpu.get_barrier_semaphore()

    def greet_s(r, carry):
        pl.semaphore_signal(barrier, inc=1, device_id=peer_s(r))
        return carry

    def greet_p(r, carry):
        pl.semaphore_signal(barrier, inc=1, device_id=peer_p(r))
        return carry

    lax.fori_loop(1, NS, greet_s, 0)
    lax.fori_loop(1, NP, greet_p, 0)

    load_x = pltpu.make_async_copy(x_hbm, xe.at[pl.ds(HALO, LX)], in_sem.at[0])
    load_p = pltpu.make_async_copy(p_hbm, pe.at[pl.ds(1, LX)], in_sem.at[1])
    load_c = pltpu.make_async_copy(c_hbm.at[s], cs.at[0], c_own)
    load_all = pltpu.make_async_copy(c_hbm, wk, in_sem.at[2])
    load_all.start()
    load_p.start()
    load_x.start()
    load_c.start()

    load_all.wait()
    row_id = lax.broadcasted_iota(jnp.int32, (M * M, NG), 0)
    sub_id = lax.broadcasted_iota(jnp.int32, (M, NG), 0)
    for chunk in range(K // NG):
        pos = modes_ref[chunk : chunk + 1, :]
        cols = slice(chunk * NG, (chunk + 1) * NG)
        upper = lax.shift_right_logical(pos, 4)
        lower = lax.bitwise_and(pos, 15)
        hot[:, cols] = jnp.where(row_id == upper, 1.0, 0.0).astype(BF16)
        low = jnp.where(sub_id == lower, 1.0, 0.0)
        lhot[:, cols] = low
        own = wk[chunk // 4, chunk % 4 : chunk % 4 + 1, :]
        for q, part in enumerate(pieces(own, 3)):
            lcs[q * M : (q + 1) * M, cols] = (low * part.astype(F32)).astype(BF16)

    pl.semaphore_wait(barrier, NS - 1 + NP - 1)

    up = {"space": jnp.minimum(s + 1, NS - 1)}
    down = {"space": jnp.maximum(s - 1, 0)}

    def remote(src, dst, send, recv, where):
        return pltpu.make_async_remote_copy(src_ref=src, dst_ref=dst, send_sem=send, recv_sem=recv, device_id=where)

    def x_up():
        return remote(x_hbm.at[pl.ds(LX - HALO, HALO)], xe.at[pl.ds(0, HALO)], halo_send.at[0], halo_recv.at[0], up)

    def x_down():
        return remote(x_hbm.at[pl.ds(0, HALO)], xe.at[pl.ds(HALO + LX, HALO)], halo_send.at[1], halo_recv.at[1], down)

    def p_up():
        return remote(p_hbm.at[pl.ds(LX - 1, 1)], pe.at[pl.ds(0, 1)], halo_send.at[2], halo_recv.at[2], up)

    def p_down():
        return remote(p_hbm.at[pl.ds(0, 1)], pe.at[pl.ds(LX + 1, 1)], halo_send.at[3], halo_recv.at[3], down)

    def r_up():
        return remote(rsum.at[pl.ds(LX, 2)], rsum.at[pl.ds(0, 2)], halo_send.at[4], halo_recv.at[4], up)

    def r_down():
        return remote(rsum.at[pl.ds(2, 2)], rsum.at[pl.ds(LX + 2, 2)], halo_send.at[5], halo_recv.at[5], down)

    @pl.when(jnp.logical_not(last))
    def _():
        x_up().start()

    @pl.when(jnp.logical_not(first))
    def _():
        x_down().start()

    @pl.when(jnp.logical_not(last))
    def _():
        p_up().start()

    @pl.when(jnp.logical_not(first))
    def _():
        p_down().start()

    def send_c(r, carry):
        remote(c_hbm.at[s], cs.at[NP - r], c_send, c_recv, peer_p(r)).start()
        return carry

    lax.fori_loop(1, NP, send_c, 0)

    @pl.when(first)
    def _():
        xe[0:HALO] = jnp.zeros((HALO, NG, NG), F32)
        pe[0:1] = jnp.zeros((1, NG, NG), F32)
        rsum[0:2] = jnp.zeros((2, 8, NG), F32)

    @pl.when(last)
    def _():
        xe[HALO + LX :] = jnp.zeros((HALO, NG, NG), F32)
        pe[LX + 1 :] = jnp.zeros((1, NG, NG), F32)
        rsum[LX + 2 :] = jnp.zeros((2, 8, NG), F32)

    flat = (
        lax.broadcasted_iota(jnp.int32, (M, NG), 0) * NG + lax.broadcasted_iota(jnp.int32, (M, NG), 1)
    )

    def sensor_of(layer, block):
        index = layer * 8 + block
        return index, sens_ref[index] - index * (M * NG)

    load_p.wait()

    def misfit(x, carry):
        for b in range(8):
            index, cell = sensor_of(s * LX + x, b)
            part = pe[x + 1, b * M : (b + 1) * M, :]
            hit = jnp.where(flat == cell, (part - obs_ref[index]) * prec_ref[index], 0.0)
            rsum[x + 2, b : b + 1, :] = jnp.sum(hit, axis=0, keepdims=True)
        return carry

    lax.fori_loop(0, LX, misfit, 0)

    @pl.when(jnp.logical_not(last))
    def _():
        r_up().start()

    @pl.when(jnp.logical_not(first))
    def _():
        r_down().start()

    eye = jnp.where(
        lax.broadcasted_iota(jnp.int32, (M, M), 0) == lax.broadcasted_iota(jnp.int32, (M, M), 1), 1.0, 0.0
    ).astype(BF16)
    by3 = pieces(by_ref[...], 3)
    bz3 = pieces(bz_ref[...], 3)
    bzt = [mm_nt(eye, part).astype(BF16) for part in bz3]
    byt = [mm_nt(eye, part).astype(BF16) for part in by3[:2]]
    for q, which in enumerate((0, 0, 1, 0, 1, 2)):
        bylhs[:, q * M : (q + 1) * M] = by3[which].astype(F32)
    lhs_y = bylhs[:, 0 : 6 * M].astype(BF16)

    xi = mm_nt(hot[...], lcs[...]).astype(BF16)
    field = mm(xi, jnp.concatenate([bzt[0]] * 3, axis=0))
    field = field + mm(xi, jnp.concatenate([bzt[1]] * 3, axis=0))
    field = field + mm(xi, jnp.concatenate([bzt[2]] * 3, axis=0))
    fbuf[...] = field.reshape(M, M, NG)

    lane = lax.broadcasted_iota(jnp.int32, (NG, NG), 1)
    suby = lax.broadcasted_iota(jnp.int32, (NG, NG), 0)
    inner_y = jnp.where(suby == NG - 1, 0.0, 0.5)
    inner_z = jnp.where(lane == NG - 1, 0.0, 0.5)
    rim = (
        jnp.where(suby == NG - 1, 1.0, 0.0)
        + jnp.where(suby == 0, 1.0, 0.0)
        + jnp.where(lane == NG - 1, 1.0, 0.0)
        + jnp.where(lane == 0, 1.0, 0.0)
    )

    def mix(e):
        g = jnp.clip(s * LX - HALO + e, 0, NX - 1)
        total = bx_ref[g, 0] * fbuf[0]
        for i in range(1, M):
            total = total + bx_ref[g, i] * fbuf[i]
        a, b, c = pieces(total, 3)
        return jnp.concatenate([a, b, a, c, b, a], axis=0)

    def faces(e, k, before):
        kp[e] = k
        ky[e] = inner_y * (k + pltpu.roll(k, NG - 1, 0))
        kz[e] = inner_z * (k + pltpu.roll(k, NG - 1, 1))
        kb[e] = rim * k
        kx[before] = 0.5 * (kp[before] + k)

    def log_layers(t, top):
        e = 2 * t
        both = jnp.exp(mm(lhs_y, jnp.concatenate([mix(e), mix(e + 1)], axis=1)))
        k0, k1 = both[:, :NG], both[:, NG:]
        faces(e, k0, jnp.maximum(e - 1, 0))
        faces(e + 1, k1, e)
        return jnp.maximum(top, jnp.max(jnp.maximum(k0, k1).reshape(NG // 8, 8, NG), axis=0))

    top = lax.fori_loop(0, HALO + LX // 2, log_layers, jnp.zeros((8, NG), F32))
    tau = (1.0 / 16.0) / jnp.max(top, keepdims=True)

    def apply(v_ref, i, e):
        v = v_ref[i]
        total = kb[e] * v
        total = total - kx[e] * (v_ref[i + 1] - v)
        total = total + kx[e - 1] * (v - v_ref[i - 1])
        fy = ky[e] * (pltpu.roll(v, NG - 1, 0) - v)
        total = total - (fy - pltpu.roll(fy, 1, 0))
        fz = kz[e] * (pltpu.roll(v, NG - 1, 1) - v)
        total = total - (fz - pltpu.roll(fz, 1, 1))
        return v, total

    def inside(g):
        return jnp.where(jnp.logical_and(g >= 0, g < NX), 1, 0)

    def put_u0(e):
        g = s * LX - 2 + e
        safe = jnp.clip(g, 0, NX - 1)
        _, image = apply(xe, e + 1, e + 1)
        load = []
        for b in range(8):
            _, cell = sensor_of(safe, b)
            load.append(jnp.where(flat == cell, rsum[e, b : b + 1, :], 0.0))
        value = jnp.concatenate(load, axis=0) - image
        u0[e] = jnp.where(inside(g) == 1, value, 0.0)

    def put_u1(e):
        g = s * LX - 1 + e
        _, image = apply(u0, e + 1, e + 2)
        u1[e] = jnp.where(inside(g) == 1, image * tau, 0.0)

    def moments(x, sums):
        second, image = apply(u1, x + 1, x + 3)
        start = u0[x + 2]
        m0, m1, m2, m3 = sums
        return (
            m0 + fold(start * start),
            m1 + fold(start * second),
            m2 + fold(second * second),
            m3 + fold(second * image),
        )

    def outer(t, count, width):
        return t + jnp.where(t >= width, count - 2 * width, 0)

    load_x.wait()
    lax.fori_loop(3, 17, lambda e, c: (put_u0(e), c)[1], 0)
    lax.fori_loop(3, 15, lambda e, c: (put_u1(e), c)[1], 0)
    zero = jnp.zeros((8, NG), F32)
    sums = lax.fori_loop(3, 13, moments, (zero, zero, zero, zero))

    @pl.when(jnp.logical_not(first))
    def _():
        x_up().wait_recv()
        r_up().wait_recv()

    @pl.when(jnp.logical_not(last))
    def _():
        x_down().wait_recv()
        r_down().wait_recv()

    lax.fori_loop(0, 6, lambda t, c: (put_u0(outer(t, LX + 4, 3)), c)[1], 0)
    lax.fori_loop(0, 6, lambda t, c: (put_u1(outer(t, LX + 2, 3)), c)[1], 0)
    sums = lax.fori_loop(0, 6, lambda t, c: moments(outer(t, LX, 3), c), sums)

    load_c.wait()
    pltpu.make_async_copy(cs.at[pl.ds(1, NP - 1)], cs.at[pl.ds(1, NP - 1)], c_recv).wait()
    every = cs[...]
    mine = cs[0]
    gap = every - mine[None]
    near = jnp.sum(jnp.sum(gap * gap, axis=1), axis=1, keepdims=True)
    center = jnp.sum(every, axis=0) * (1.0 / NP)
    off = every - center[None]
    spread = jnp.sum(jnp.sum(off * off, axis=0), keepdims=True) * (2.0 / (NP - 1))
    lane32 = lax.broadcasted_iota(jnp.int32, (NP, NG), 1)
    diag = lane32 == lax.broadcasted_iota(jnp.int32, (NP, NG), 0)
    near_row = jnp.sum(jnp.where(diag, near, 0.0), axis=0, keepdims=True)
    near_row = jnp.where(lane32[0:1] == NP, spread, near_row)

    m3 = sums[3] * tau
    rows = [jnp.sum(m, axis=0, keepdims=True) for m in (sums[0], sums[1], sums[2], m3)]
    blank = jnp.zeros((2, NG), F32)
    mom[0] = jnp.concatenate(rows + [jnp.broadcast_to(tau, (1, NG)), near_row, blank], axis=0)

    def send_m(r, carry):
        remote(mom.at[0], mom.at[NS - r], m_send, m_recv, peer_s(r)).start()
        return carry

    lax.fori_loop(1, NS, send_m, 0)
    pltpu.make_async_copy(mom.at[pl.ds(1, NS - 1)], mom.at[pl.ds(1, NS - 1)], m_recv).wait()

    taus = mom[:, 4:5, :]
    least = jnp.min(taus, axis=0)
    ratio = least[None] / taus
    q0 = jnp.sum(jnp.sum(mom[:, 0:1, :], axis=0), axis=1, keepdims=True)
    q1 = jnp.sum(jnp.sum(mom[:, 1:2, :] * ratio, axis=0), axis=1, keepdims=True)
    q2 = jnp.sum(jnp.sum(mom[:, 2:3, :] * ratio * ratio, axis=0), axis=1, keepdims=True)
    q3 = jnp.sum(jnp.sum(mom[:, 3:4, :] * ratio * ratio * ratio, axis=0), axis=1, keepdims=True)
    alpha = q0 / q1
    norm = alpha * alpha * q2 - q0
    grown = norm / q0 + 1.0
    alpha1 = norm / (alpha * alpha * (q3 - q2 * (q2 / q1)))
    tau0 = least[:, 0:1]
    scale0 = tau0 * (alpha + alpha1 * grown)
    scale1 = -(tau0 * alpha1) * (alpha * (tau0 / tau))

    def put_x(e, carry):
        xo[e] = xe[e + 2] + scale0 * u0[e + 1] + scale1 * u1[e]
        return carry

    lax.fori_loop(0, LX + 2, put_x, 0)
    store = pltpu.make_async_copy(xo.at[pl.ds(1, LX)], adj_hbm, out_sem)
    store.start()

    @pl.when(jnp.logical_not(first))
    def _():
        p_up().wait_recv()

    @pl.when(jnp.logical_not(last))
    def _():
        p_down().wait_recv()

    lhs_p = jnp.concatenate(
        [jnp.concatenate([byt[0], byt[0]], axis=1), jnp.concatenate([byt[1], byt[1]], axis=1)], axis=0
    )

    def cell_grad(x):
        a, p = xo[x + 1], pe[x + 1]
        upper = jnp.where(jnp.logical_and(last, x == LX - 1), 1.0, 0.5)
        lower = jnp.where(jnp.logical_and(first, x == 0), 1.0, 0.5)
        total = rim * (a * p)
        total = total + upper * ((xo[x + 2] - a) * (pe[x + 2] - p))
        total = total + lower * ((a - xo[x]) * (p - pe[x]))
        qy = inner_y * ((pltpu.roll(a, NG - 1, 0) - a) * (pltpu.roll(p, NG - 1, 0) - p))
        total = total + (qy + pltpu.roll(qy, 1, 0))
        qz = inner_z * ((pltpu.roll(a, NG - 1, 1) - a) * (pltpu.roll(p, NG - 1, 1) - p))
        total = total + (qz + pltpu.roll(qz, 1, 1))
        return jnp.concatenate(pieces(kp[x + HALO] * total, 2), axis=0)

    def proj_layers(t, carry):
        x = 2 * t
        got = mm(lhs_p, jnp.concatenate([cell_grad(x), cell_grad(x + 1)], axis=1))
        got = got[:M] + got[M:]
        pbuf[x] = got[:, :NG]
        pbuf[x + 1] = got[:, NG:]
        return carry

    lax.fori_loop(0, LX // 2, proj_layers, 0)

    def mix_x(i, carry):
        total = bx_ref[s * LX, i] * pbuf[0]
        for x in range(1, LX):
            total = total + bx_ref[s * LX + x, i] * pbuf[x]
        qbuf[i] = total
        return carry

    lax.fori_loop(0, M, mix_x, 0)
    q_two = jnp.concatenate(pieces(qbuf[...].reshape(M * M, NG), 2), axis=1)
    lhs_z = jnp.concatenate(
        [jnp.concatenate([bzt[0], bzt[0]], axis=1), jnp.concatenate([bzt[1], bzt[1]], axis=1)], axis=0
    )
    tensor = mm_nt(lhs_z, q_two)
    tensor = tensor[:M] + tensor[M:]
    rhs = jnp.concatenate(pieces(tensor, 3), axis=0)

    def share_out(r, carry):
        share = lax.rem(s + r, NS)
        cols = pl.ds(pl.multiple_of(share * SH, SH), SH)
        got = mm(rhs, hot[:, cols])
        got = (got[:M] + got[M : 2 * M] + got[2 * M :]) * lhot[:, cols]
        row = jnp.sum(got, axis=0, keepdims=True)
        for q in range(SH // NG):
            pk[r, q : q + 1, :] = row[:, q * NG : (q + 1) * NG]
        return carry

    def share_send(r, carry):
        share_out(r, carry)
        remote(pk.at[r], rp.at[NS - r], r_send, r_recv, peer_s(r)).start()
        return carry

    lax.fori_loop(1, NS, share_send, 0)
    share_out(0, 0)

    near_all = jnp.sum(mom[:, 5:6, :], axis=0)
    width = near_all[:, NP : NP + 1]
    kern = jnp.exp(-near_all / width)
    kcol = jnp.sum(jnp.where(diag, kern, 0.0), axis=1, keepdims=True)
    weight = jnp.broadcast_to(kcol[:, :, None], (NP, 1, NG))
    drive = jnp.sum(weight * every, axis=0)
    repel = jnp.sum(weight * (mine[None] - every), axis=0)
    base = mine + (STEP / NP) * ((2.0 / width) * repel - drive)

    pltpu.make_async_copy(rp.at[pl.ds(1, NS - 1)], rp.at[pl.ds(1, NS - 1)], r_recv).wait()
    total = pk[0]
    for r in range(1, NS):
        total = total + rp[r]
    gs[0] = total

    def send_g(r, carry):
        remote(gs.at[0], gs.at[NP - r], g_send, g_recv, peer_p(r)).start()
        return carry

    lax.fori_loop(1, NP, send_g, 0)
    pltpu.make_async_copy(gs.at[pl.ds(1, NP - 1)], gs.at[pl.ds(1, NP - 1)], g_recv).wait()
    new_ref[...] = base - (STEP / NP) * jnp.sum(weight * gs[...], axis=0)

    def sent(ref, sem):
        pltpu.make_async_copy(ref, ref, sem).wait()

    sent(cs.at[pl.ds(1, NP - 1)], c_send)
    sent(mom.at[pl.ds(1, NS - 1)], m_send)
    sent(rp.at[pl.ds(1, NS - 1)], r_send)
    sent(gs.at[pl.ds(1, NP - 1)], g_send)

    @pl.when(jnp.logical_not(last))
    def _():
        x_up().wait_send()
        p_up().wait_send()
        r_up().wait_send()

    @pl.when(jnp.logical_not(first))
    def _():
        x_down().wait_send()
        p_down().wait_send()
        r_down().wait_send()

    store.wait()


def shards(coeffs, modes, basis_x, basis_y, basis_z, pressure, initial_adjoint, sensors, observed, precision):
    vmem = pl.BlockSpec(memory_space=pltpu.VMEM)
    smem = pl.BlockSpec(memory_space=pltpu.SMEM)
    anywhere = pl.BlockSpec(memory_space=pl.ANY)
    dma = pltpu.SemaphoreType.DMA
    layers = lambda count: pltpu.VMEM((count, NG, NG), F32)
    new, adjoint = pl.pallas_call(
        kernel,
        out_shape=(
            jax.ShapeDtypeStruct((SH // NG, NG), F32),
            jax.ShapeDtypeStruct((LX, NG, NG), F32),
        ),
        in_specs=[anywhere, vmem, smem, vmem, vmem, anywhere, anywhere, smem, smem, smem],
        out_specs=(vmem, anywhere),
        scratch_shapes=[
            layers(LX + 6),
            layers(LX + 2),
            layers(LX + 6),
            layers(LX + 6),
            layers(LX + 6),
            layers(LX + 6),
            layers(LX + 6),
            layers(LX + 4),
            layers(LX + 2),
            layers(LX + 2),
            pltpu.VMEM((LX + 4, 8, NG), F32),
            pltpu.VMEM((M * M, K), BF16),
            pltpu.VMEM((M, K), F32),
            pltpu.VMEM((3 * M, K), BF16),
            pltpu.VMEM((NG, NG), F32),
            pltpu.VMEM((M, M, NG), F32),
            pltpu.VMEM((LX, M, NG), F32),
            pltpu.VMEM((M, M, NG), F32),
            pltpu.VMEM((NP, SH // NG, NG), F32),
            pltpu.VMEM((NS, SH // NG, NG), F32),
            pltpu.VMEM((NS, SH // NG, NG), F32),
            pltpu.VMEM((NS, SH // NG, NG), F32),
            pltpu.VMEM((NP, SH // NG, NG), F32),
            pltpu.VMEM((NS, 8, NG), F32),
            dma((3,)), dma, dma((6,)), dma((6,)),
            dma, dma, dma, dma, dma, dma, dma, dma, dma,
        ],
        compiler_params=pltpu.CompilerParams(
            collective_id=0, has_side_effects=True, vmem_limit_bytes=48 * 2**20
        ),
    )(
        coeffs.reshape(NS, SH // NG, NG),
        modes.reshape(K // NG, NG),
        basis_x,
        basis_y,
        basis_z,
        pressure[0],
        initial_adjoint[0],
        sensors,
        observed,
        precision,
    )
    return new.reshape(1, SH), adjoint[None]


def solution(mesh):
    in_specs = (
        P("particle", None),
        P(),
        P(),
        P(),
        P(),
        P("particle", "space", None, None),
        P("particle", "space", None, None),
        P(),
        P(),
        P(),
    )
    out_specs = (P("particle", "space"), P("particle", "space", None, None))
    return jax.shard_map(shards, mesh=mesh, in_specs=in_specs, out_specs=out_specs, check_vma=False)
```

time: 331 us -> 53 us (0.16)
  blocking collectives: 191 us -> 0 us
  local copies, waits for them, and re-layouts: 60.1 us -> 6.23 us
  Pallas kernels: 0 us -> 45.7 us
  other arithmetic: 39.3 us -> 0 us
  starting transfers between devices: 22.1 us -> 0 us
  matrix products: 10.4 us -> 0 us
  between operations: 5.77 us -> 0.68 us
    psum x4 -> x0, blocking collectives: 97.6 us -> none  [the longest x1 34.3 us: shards(): summed = lax.psum(partial_value, 'space')]
    all_gather x2 -> x0, blocking collectives: 93.2 us -> none  [the longest x1 53.4 us: shards(): lax.all_gather(grad[None], 'particle', axis=0, tiled=True)]
    pallas_call x0 -> x1, Pallas kernels: none -> 45.7 us  [shards(): pl.pallas_call(kernel, out_shape=(jax.ShapeDtypeStruct((SH // NG, NG), F3...]
    gather x3 -> x0, local copies, waits for them, and re-layouts: 29.7 us -> none  [the longest x1 23 us: shards(): partial_value = project(cellgrad, local_rows, basis_y, basis_z)[modes]]
    ppermute x8 -> x0, starting transfers between devices: 22.1 us -> none  [the longest x4 16.6 us: padded(): before = lax.ppermute(last, axis, up)]
    scatter x1 -> x0, local copies, waits for them, and re-layouts: 15.7 us -> none  [log_field(): flat = jnp.zeros((msize * msize * msize,), jnp.float32).at[modes].set(xi)]
    dot_general x8 -> x0, matrix products: 10.4 us -> none  [the longest x1 3.07 us: project(): first = jnp.einsum('xyz,zl->xyl', cellgrad, basis_z, precision=HIGH)]
    reduce_sum x6 -> x0, other arithmetic: 10.4 us -> none  [the longest x2 6.26 us: shards(): alpha = norm_now / lax.psum(jnp.sum(direction * image), 'space')]
  transfers between devices with their start and end apart: 8 -> 0, of which waited for: 1 -> 0; matrix products, arithmetic and copies ran while one was open for 14% -> 0% of each run, Pallas kernels for 0% -> 0%
where the time goes in v1:
time: 53 us; the launch traced here: 52.6 us
  Pallas kernels  45.7 us (86%)
  local copies, waits for them, and re-layouts  6.23 us (12%)
  between operations  0.68 us (1%)
    pallas_call x1, Pallas kernels, shards(): pl.pallas_call(kernel, out_shape=(jax.ShapeDtypeStruct((SH // NG, NG), F3...  45.7 us
    unnamed x23, local copies, waits for them, and re-layouts  6.23 us

profile of v1, /device:TPU:1, one launch (start us, length us, event | category | flops | bytes accessed | tf_op | source)
XLA Modules:
  0.0 52.6 jit_solution(11689721348545372468)
XLA Ops:
  0.6 0.0 copy-start.7
  0.6 0.8 %copy.12.bx_ref = f32[128,16]{1,0:T(8,128)S(1)} copy(f32[128,16]{0,1:T(8,128)} %param.12) | data formatting | bytes 16384 | tf_op args[2]
  1.4 0.0 copy-done.7
  1.4 0.0 copy-start.8
  1.5 0.1 copy.13.by_ref
  1.6 0.6 %copy-done.8 = f32[128,16]{0,1:T(8,128)S(1)} copy-done((f32[128,16]{0,1:T(8,128)S(1)}, f32[128,16]{0,1:T(8,128)}, u32[]{:S(2)}) %copy-start.8) | copy-done | bytes 8216
  2.1 0.0 copy-start.2
  2.1 0.0 copy-start.3
  2.2 0.0 copy-start.4
  2.2 0.0 copy-start.5
  2.2 0.0 copy-start.6
  2.2 0.1 copy.14.bz_ref
  2.3 0.6 %copy-done.2 = f32[1,4096]{1,0:T(1,128)S(1)} copy-done((f32[1,4096]{1,0:T(1,128)S(1)}, f32[1,4096]{1,0:T(1,128)}, u32[]{:S(2)}) %copy-start.2) | copy-done | bytes 16408
  2.9 0.0 copy-done.3
  2.9 0.0 copy-done.4
  2.9 0.0 copy-done.5
  2.9 0.0 copy-done.6
  2.9 0.0 copy-start
  2.9 1.2 %copy-done = f32[1,16,128,128]{3,2,1,0:T(8,128)S(1)} copy-done((f32[1,16,128,128]{3,2,1,0:T(8,128)S(1)}, f32[1,16,128,128]{3,2,1,0:T(8,128)}, u32[]{:S(2)}) %copy-start) | copy-done | bytes 1048600
  4.1 0.0 copy-start.1
  4.1 1.2 %copy-done.1 = f32[1,16,128,128]{3,2,1,0:T(8,128)S(1)} copy-done((f32[1,16,128,128]{3,2,1,0:T(8,128)S(1)}, f32[1,16,128,128]{3,2,1,0:T(8,128)}, u32[]{:S(2)}) %copy-start.1) | copy-done | bytes 1048600
  5.4 45.7 %shard_map.113 = (f32[4,128]{1,0:T(4,128)S(1)}, f32[16,128,128]{2,1,0:T(8,128)S(1)}) custom-call(f32[8,4,128]{2,1,0:T(4,128)S(1)} %bitcast.9, s32[32,128]{1,0:T(8,128)S(1)} %bitcast.10, f32[128,16]{1,0:T(8,128)S(1)} %copy.12.bx_ref, f32[128,16]{1,0:T(8,128)S(1)} %copy.13.by_ref, f32[128,16]{1,0:T(8,128)S(1)} %copy.14.bz_ref, f32[16,128,128]{2,1,0:T(8,128)S(1)} %bitcast.6, ...), custom_call_target="tpu_custom_call" | custom-call | tf_op jit(solution)/shard_map/pallas_call | solution.py:476
  51.1 0.6 %copy.17 = f32[1,512]{1,0:T(1,128)} copy(f32[1,512]{1,0:T(1,128)S(1)} %bitcast.11) | data formatting | bytes 4096
  51.7 1.0 %copy.18 = f32[1,16,128,128]{3,2,1,0:T(8,128)} copy(f32[1,16,128,128]{3,2,1,0:T(8,128)S(1)} %bitcast.8) | data formatting | bytes 2097152
Async XLA Ops:
  0.6 0.8 %copy-start.7 = (f32[128,16]{0,1:T(8,128)S(1)}, f32[128,16]{0,1:T(8,128)}, u32[]{:S(2)}) copy-start(f32[128,16]{0,1:T(8,128)} %param.13) | copy-start | bytes 24580
  1.4 0.7 %copy-start.8 = (f32[128,16]{0,1:T(8,128)S(1)}, f32[128,16]{0,1:T(8,128)}, u32[]{:S(2)}) copy-start(f32[128,16]{0,1:T(8,128)} %param.14) | copy-start | bytes 24580
  2.1 0.7 %copy-start.2 = (f32[1,4096]{1,0:T(1,128)S(1)}, f32[1,4096]{1,0:T(1,128)}, u32[]{:S(2)}) copy-start(f32[1,4096]{1,0:T(1,128)} %param.10) | copy-start | bytes 49156
  2.1 0.7 %copy-start.3 = (s32[4096]{0:T(1024)S(1)}, s32[4096]{0:T(1024)}, u32[]{:S(2)}) copy-start(s32[4096]{0:T(1024)} %param.11) | copy-start | bytes 49156
  2.2 0.7 %copy-start.4 = (s32[1024]{0:T(1024)S(1)}, s32[1024]{0:T(1024)}, u32[]{:S(2)}) copy-start(s32[1024]{0:T(1024)} %sens_ref.1) | copy-start | bytes 12292
  2.2 0.7 %copy-start.5 = (f32[1024]{0:T(1024)S(1)}, f32[1024]{0:T(1024)}, u32[]{:S(2)}) copy-start(f32[1024]{0:T(1024)} %obs_ref.1) | copy-start | bytes 12292
  2.2 0.7 %copy-start.6 = (f32[1024]{0:T(1024)S(1)}, f32[1024]{0:T(1024)}, u32[]{:S(2)}) copy-start(f32[1024]{0:T(1024)} %prec_ref.1) | copy-start | bytes 12292
  2.9 1.2 %copy-start = (f32[1,16,128,128]{3,2,1,0:T(8,128)S(1)}, f32[1,16,128,128]{3,2,1,0:T(8,128)}, u32[]{:S(2)}) copy-start(f32[1,16,128,128]{3,2,1,0:T(8,128)} %param.15) | copy-start | bytes 3145732
  4.1 1.2 %copy-start.1 = (f32[1,16,128,128]{3,2,1,0:T(8,128)S(1)}, f32[1,16,128,128]{3,2,1,0:T(8,128)}, u32[]{:S(2)}) copy-start(f32[1,16,128,128]{3,2,1,0:T(8,128)} %param.16) | copy-start | bytes 3145732

commit v2 on v1

--- a/solution.py
+++ b/solution.py
@@ -45,7 +45,7 @@
 def kernel(
     c_hbm, modes_ref, bx_ref, by_ref, bz_ref, p_hbm, x_hbm, sens_ref, obs_ref, prec_ref,
     new_ref, adj_hbm,
-    xe, pe, kp, kx, ky, kz, kb, u0, u1, xo, rsum, hot, lhot, lcs, bylhs, fbuf, pbuf, qbuf,
+    xe, pe, kp, kx, ky, kz, kb, u0, u1, xo, rsum, hot, lhot, lcs, fbuf, pbuf, qbuf,
     cs, wk, pk, rp, gs, mom,
     in_sem, out_sem, halo_send, halo_recv, c_own, c_send, c_recv, m_send, m_recv, r_send, r_recv, g_send, g_recv,
 ):
@@ -185,16 +185,12 @@
     def _():
         r_down().start()
 
-    eye = jnp.where(
-        lax.broadcasted_iota(jnp.int32, (M, M), 0) == lax.broadcasted_iota(jnp.int32, (M, M), 1), 1.0, 0.0
-    ).astype(BF16)
-    by3 = pieces(by_ref[...], 3)
-    bz3 = pieces(bz_ref[...], 3)
-    bzt = [mm_nt(eye, part).astype(BF16) for part in bz3]
-    byt = [mm_nt(eye, part).astype(BF16) for part in by3[:2]]
-    for q, which in enumerate((0, 0, 1, 0, 1, 2)):
-        bylhs[:, q * M : (q + 1) * M] = by3[which].astype(F32)
-    lhs_y = bylhs[:, 0 : 6 * M].astype(BF16)
+    lane = lax.broadcasted_iota(jnp.int32, (NG, NG), 1)
+    suby = lax.broadcasted_iota(jnp.int32, (NG, NG), 0)
+    eye = jnp.where(lane == suby, 1.0, 0.0).astype(BF16)
+    byt = pieces(by_ref[...], 3)
+    bzt = pieces(bz_ref[...], 3)
+    lhs_y = mm_nt(eye, jnp.concatenate([byt[which] for which in (0, 0, 1, 0, 1, 2)], axis=0)).astype(BF16)
 
     xi = mm_nt(hot[...], lcs[...]).astype(BF16)
     field = mm(xi, jnp.concatenate([bzt[0]] * 3, axis=0))
@@ -202,8 +198,6 @@
     field = field + mm(xi, jnp.concatenate([bzt[2]] * 3, axis=0))
     fbuf[...] = field.reshape(M, M, NG)
 
-    lane = lax.broadcasted_iota(jnp.int32, (NG, NG), 1)
-    suby = lax.broadcasted_iota(jnp.int32, (NG, NG), 0)
     inner_y = jnp.where(suby == NG - 1, 0.0, 0.5)
     inner_z = jnp.where(lane == NG - 1, 0.0, 0.5)
     rim = (
@@ -215,9 +209,9 @@
 
     def mix(e):
         g = jnp.clip(s * LX - HALO + e, 0, NX - 1)
-        total = bx_ref[g, 0] * fbuf[0]
+        total = bx_ref[0, g] * fbuf[0]
         for i in range(1, M):
-            total = total + bx_ref[g, i] * fbuf[i]
+            total = total + bx_ref[i, g] * fbuf[i]
         a, b, c = pieces(total, 3)
         return jnp.concatenate([a, b, a, c, b, a], axis=0)
 
@@ -388,9 +382,9 @@
     lax.fori_loop(0, LX // 2, proj_layers, 0)
 
     def mix_x(i, carry):
-        total = bx_ref[s * LX, i] * pbuf[0]
+        total = bx_ref[i, s * LX] * pbuf[0]
         for x in range(1, LX):
-            total = total + bx_ref[s * LX + x, i] * pbuf[x]
+            total = total + bx_ref[i, s * LX + x] * pbuf[x]
         qbuf[i] = total
         return carry
 
@@ -496,7 +490,6 @@
             pltpu.VMEM((M * M, K), BF16),
             pltpu.VMEM((M, K), F32),
             pltpu.VMEM((3 * M, K), BF16),
-            pltpu.VMEM((NG, NG), F32),
             pltpu.VMEM((M, M, NG), F32),
             pltpu.VMEM((LX, M, NG), F32),
             pltpu.VMEM((M, M, NG), F32),
@@ -510,14 +503,14 @@
             dma, dma, dma, dma, dma, dma, dma, dma, dma,
         ],
         compiler_params=pltpu.CompilerParams(
-            collective_id=0, has_side_effects=True, vmem_limit_bytes=48 * 2**20
+            collective_id=0, has_side_effects=True, vmem_limit_bytes=60 * 2**20
         ),
     )(
         coeffs.reshape(NS, SH // NG, NG),
         modes.reshape(K // NG, NG),
-        basis_x,
-        basis_y,
-        basis_z,
+        basis_x.T,
+        basis_y.T,
+        basis_z.T,
         pressure[0],
         initial_adjoint[0],
         sensors,

time: 53 us -> 50.1 us (0.945)
  local copies, waits for them, and re-layouts: 6.23 us -> 3.52 us
    unnamed x23 -> x4, local copies, waits for them, and re-layouts: 6.23 us -> 3.52 us
where the time goes in v2:
time: 50.1 us; the launch traced here: 49.9 us
  Pallas kernels  45.7 us (91%)
  local copies, waits for them, and re-layouts  3.52 us (7%)
  between operations  0.65 us (1%)
    pallas_call x1, Pallas kernels, shards(): pl.pallas_call(kernel, out_shape=(jax.ShapeDtypeStruct((SH // NG, NG), F3...  45.7 us
    unnamed x4, local copies, waits for them, and re-layouts  3.52 us

profile of v2, /device:TPU:1, one launch (start us, length us, event | category | flops | bytes accessed | tf_op | source)
XLA Modules:
  0.0 49.9 jit_solution(7039683985950653762)
XLA Ops:
  0.6 45.7 %shard_map.113 = (f32[4,128]{1,0:T(4,128)}, f32[16,128,128]{2,1,0:T(8,128)}) custom-call(f32[8,4,128]{2,1,0:T(4,128)} %bitcast.12, s32[32,128]{1,0:T(8,128)} %bitcast.13, f32[16,128]{1,0:T(8,128)} %bitcast.14, f32[16,128]{1,0:T(8,128)} %bitcast.15, f32[16,128]{1,0:T(8,128)} %bitcast.16, f32[16,128,128]{2,1,0:T(8,128)} %bitcast.9, f32[16,128,128]{2,1,0:T(8,128)} %bitcast.10, ...), custom_call_target="tpu_custom_call" | custom-call | tf_op jit(solution)/shard_map/pallas_call | solution.py:470
  46.4 0.0 copy-start
  46.4 0.6 %copy-done = f32[4,128]{1,0:T(4,128)S(1)} copy-done((f32[4,128]{1,0:T(4,128)S(1)}, f32[4,128]{1,0:T(4,128)}, u32[]{:S(2)}) %copy-start) | copy-done | bytes 2072
  47.0 0.6 %copy.14 = f32[1,512]{1,0:T(1,128)} copy(f32[1,512]{1,0:T(1,128)S(1)} %bitcast.17) | data formatting | bytes 4096
  47.6 2.3 %copy.15 = f32[1,16,128,128]{3,2,1,0:T(8,128)} copy(f32[1,16,128,128]{3,2,1,0:T(8,128)} %bitcast.11) | data formatting | bytes 2097152
Async XLA Ops:
  46.4 0.7 %copy-start = (f32[4,128]{1,0:T(4,128)S(1)}, f32[4,128]{1,0:T(4,128)}, u32[]{:S(2)}) copy-start(f32[4,128]{1,0:T(4,128)} %get-tuple-element.4) | copy-start | bytes 6148

commit v3 on v2

v3 whole, which is shorter than its diff:
```python
import jax
import jax.numpy as jnp
from jax import lax
from jax.experimental import pallas as pl
from jax.experimental.pallas import tpu as pltpu
from jax.sharding import PartitionSpec as P

F32 = jnp.float32
BF16 = jnp.bfloat16
NP = 32
NS = 8
LX = 16
NX = 128
NG = 128
M = 16
K = M * M * M
SH = K // NS
HALO = 3
STEP = 0.5
NN = (((1,), (1,)), ((), ()))


def pieces(value, count):
    out = []
    rest = value
    for _ in range(count):
        part = rest.astype(BF16)
        out.append(part)
        rest = rest - part.astype(F32)
    return out


def mm(a, b):
    return jnp.dot(a, b, preferred_element_type=F32)


def mm_nt(a, b):
    return lax.dot_general(a, b, NN, preferred_element_type=F32)


def fold(value):
    return jnp.sum(value.reshape(NG // 8, 8, NG), axis=0)


def kernel(
    c_hbm, modes_ref, bx_ref, by_ref, bz_ref, p_hbm, x_hbm, sens_ref, obs_ref, prec_ref,
    new_ref, adj_hbm,
    xe, pe, kp, kx, ky, kz, kb, u0, u1, xo, rsum, hot, lhot, lcs, fbuf, pbuf, qbuf,
    cs, wk, pk, rp, gs,
    in_sem, out_sem, halo_send, halo_recv, c_own, c_send, c_recv, r_send, r_recv, g_send, g_recv,
):
    n = lax.axis_index("particle")
    s = lax.axis_index("space")
    first = s == 0
    last = s == NS - 1

    def peer_p(r):
        return {"particle": lax.rem(n + r, NP)}

    def peer_s(r):
        return {"space": lax.rem(s + r, NS)}

    barrier = pltpu.get_barrier_semaphore()

    def greet_s(r, carry):
        pl.semaphore_signal(barrier, inc=1, device_id=peer_s(r))
        return carry

    def greet_p(r, carry):
        pl.semaphore_signal(barrier, inc=1, device_id=peer_p(r))
        return carry

    lax.fori_loop(1, NS, greet_s, 0)
    lax.fori_loop(1, NP, greet_p, 0)

    load_x = pltpu.make_async_copy(x_hbm, xe.at[pl.ds(HALO, LX)], in_sem.at[0])
    load_p = pltpu.make_async_copy(p_hbm, pe.at[pl.ds(1, LX)], in_sem.at[1])
    load_c = pltpu.make_async_copy(c_hbm.at[s], cs.at[0], c_own)
    load_all = pltpu.make_async_copy(c_hbm, wk, in_sem.at[2])
    load_all.start()
    load_p.start()
    load_x.start()
    load_c.start()

    load_all.wait()
    row_id = lax.broadcasted_iota(jnp.int32, (M * M, NG), 0)
    sub_id = lax.broadcasted_iota(jnp.int32, (M, NG), 0)
    for chunk in range(K // NG):
        pos = modes_ref[chunk : chunk + 1, :]
        cols = slice(chunk * NG, (chunk + 1) * NG)
        upper = lax.shift_right_logical(pos, 4)
        lower = lax.bitwise_and(pos, 15)
        hot[:, cols] = jnp.where(row_id == upper, 1.0, 0.0).astype(BF16)
        low = jnp.where(sub_id == lower, 1.0, 0.0)
        lhot[:, cols] = low
        own = wk[chunk // 4, chunk % 4 : chunk % 4 + 1, :]
        for q, part in enumerate(pieces(own, 3)):
            lcs[q * M : (q + 1) * M, cols] = (low * part.astype(F32)).astype(BF16)

    lane = lax.broadcasted_iota(jnp.int32, (NG, NG), 1)
    suby = lax.broadcasted_iota(jnp.int32, (NG, NG), 0)
    eye = jnp.where(lane == suby, 1.0, 0.0).astype(BF16)
    byt = pieces(by_ref[...], 3)
    bzt = pieces(bz_ref[...], 3)
    lhs_y = mm_nt(eye, jnp.concatenate([byt[which] for which in (0, 0, 1, 0, 1, 2)], axis=0)).astype(BF16)

    xi = mm_nt(hot[...], lcs[...]).astype(BF16)
    field = mm(xi, jnp.concatenate([bzt[0]] * 3, axis=0))
    field = field + mm(xi, jnp.concatenate([bzt[1]] * 3, axis=0))
    field = field + mm(xi, jnp.concatenate([bzt[2]] * 3, axis=0))
    fbuf[...] = field.reshape(M, M, NG)

    inner_y = jnp.where(suby == NG - 1, 0.0, 0.5)
    inner_z = jnp.where(lane == NG - 1, 0.0, 0.5)
    rim = (
        jnp.where(suby == NG - 1, 1.0, 0.0)
        + jnp.where(suby == 0, 1.0, 0.0)
        + jnp.where(lane == NG - 1, 1.0, 0.0)
        + jnp.where(lane == 0, 1.0, 0.0)
    )

    def mix(e):
        g = jnp.clip(s * LX - HALO + e, 0, NX - 1)
        total = bx_ref[0, g] * fbuf[0]
        for i in range(1, M):
            total = total + bx_ref[i, g] * fbuf[i]
        a, b, c = pieces(total, 3)
        return jnp.concatenate([a, b, a, c, b, a], axis=0)

    def faces(e, k, before):
        kp[e] = k
        ky[e] = inner_y * (k + pltpu.roll(k, NG - 1, 0))
        kz[e] = inner_z * (k + pltpu.roll(k, NG - 1, 1))
        kb[e] = rim * k
        kx[before] = 0.5 * (kp[before] + k)

    def log_layers(t, top):
        e = 2 * t
        both = jnp.exp(mm(lhs_y, jnp.concatenate([mix(e), mix(e + 1)], axis=1)))
        k0, k1 = both[:, :NG], both[:, NG:]
        faces(e, k0, jnp.maximum(e - 1, 0))
        faces(e + 1, k1, e)
        return jnp.maximum(top, jnp.max(jnp.maximum(k0, k1).reshape(NG // 8, 8, NG), axis=0))

    top = lax.fori_loop(0, HALO + LX // 2, log_layers, jnp.zeros((8, NG), F32))
    tau = (1.0 / 16.0) / jnp.max(top, keepdims=True)

    @pl.when(first)
    def _():
        xe[0:HALO] = jnp.zeros((HALO, NG, NG), F32)
        pe[0:1] = jnp.zeros((1, NG, NG), F32)
        rsum[0:2] = jnp.zeros((2, 8, NG), F32)

    @pl.when(last)
    def _():
        xe[HALO + LX :] = jnp.zeros((HALO, NG, NG), F32)
        pe[LX + 1 :] = jnp.zeros((1, NG, NG), F32)
        rsum[LX + 2 :] = jnp.zeros((2, 8, NG), F32)

    flat = (
        lax.broadcasted_iota(jnp.int32, (M, NG), 0) * NG + lax.broadcasted_iota(jnp.int32, (M, NG), 1)
    )

    def sensor_of(layer, block):
        index = layer * 8 + block
        return index, sens_ref[index] - index * (M * NG)

    load_p.wait()

    def misfit(x, carry):
        for b in range(8):
            index, cell = sensor_of(s * LX + x, b)
            part = pe[x + 1, b * M : (b + 1) * M, :]
            hit = jnp.where(flat == cell, (part - obs_ref[index]) * prec_ref[index], 0.0)
            rsum[x + 2, b : b + 1, :] = jnp.sum(hit, axis=0, keepdims=True)
        return carry

    lax.fori_loop(0, LX, misfit, 0)

    pl.semaphore_wait(barrier, NS - 1 + NP - 1)

    up = {"space": jnp.minimum(s + 1, NS - 1)}
    down = {"space": jnp.maximum(s - 1, 0)}

    def remote(src, dst, send, recv, where):
        return pltpu.make_async_remote_copy(src_ref=src, dst_ref=dst, send_sem=send, recv_sem=recv, device_id=where)

    def x_up():
        return remote(x_hbm.at[pl.ds(LX - HALO, HALO)], xe.at[pl.ds(0, HALO)], halo_send.at[0], halo_recv.at[0], up)

    def x_down():
        return remote(x_hbm.at[pl.ds(0, HALO)], xe.at[pl.ds(HALO + LX, HALO)], halo_send.at[1], halo_recv.at[1], down)

    def p_up():
        return remote(p_hbm.at[pl.ds(LX - 1, 1)], pe.at[pl.ds(0, 1)], halo_send.at[2], halo_recv.at[2], up)

    def p_down():
        return remote(p_hbm.at[pl.ds(0, 1)], pe.at[pl.ds(LX + 1, 1)], halo_send.at[3], halo_recv.at[3], down)

    def r_up():
        return remote(rsum.at[pl.ds(LX, 2)], rsum.at[pl.ds(0, 2)], halo_send.at[4], halo_recv.at[4], up)

    def r_down():
        return remote(rsum.at[pl.ds(2, 2)], rsum.at[pl.ds(LX + 2, 2)], halo_send.at[5], halo_recv.at[5], down)

    @pl.when(jnp.logical_not(last))
    def _():
        x_up().start()

    @pl.when(jnp.logical_not(first))
    def _():
        x_down().start()

    @pl.when(jnp.logical_not(last))
    def _():
        p_up().start()

    @pl.when(jnp.logical_not(first))
    def _():
        p_down().start()

    def send_c(r, carry):
        remote(c_hbm.at[s], cs.at[NP - r], c_send, c_recv, peer_p(r)).start()
        return carry

    @pl.when(jnp.logical_not(last))
    def _():
        r_up().start()

    @pl.when(jnp.logical_not(first))
    def _():
        r_down().start()

    lax.fori_loop(1, NP, send_c, 0)

    def apply(v_ref, i, e):
        v = v_ref[i]
        total = kb[e] * v
        total = total - kx[e] * (v_ref[i + 1] - v)
        total = total + kx[e - 1] * (v - v_ref[i - 1])
        fy = ky[e] * (pltpu.roll(v, NG - 1, 0) - v)
        total = total - (fy - pltpu.roll(fy, 1, 0))
        fz = kz[e] * (pltpu.roll(v, NG - 1, 1) - v)
        total = total - (fz - pltpu.roll(fz, 1, 1))
        return v, total

    def inside(g):
        return jnp.where(jnp.logical_and(g >= 0, g < NX), 1, 0)

    def put_u0(e):
        g = s * LX - 2 + e
        safe = jnp.clip(g, 0, NX - 1)
        _, image = apply(xe, e + 1, e + 1)
        load = []
        for b in range(8):
            _, cell = sensor_of(safe, b)
            load.append(jnp.where(flat == cell, rsum[e, b : b + 1, :], 0.0))
        value = jnp.concatenate(load, axis=0) - image
        u0[e] = jnp.where(inside(g) == 1, value, 0.0)

    def put_u1(e):
        g = s * LX - 1 + e
        _, image = apply(u0, e + 1, e + 2)
        u1[e] = jnp.where(inside(g) == 1, image * tau, 0.0)

    def moments(x, sums):
        second, image = apply(u1, x + 1, x + 3)
        start = u0[x + 2]
        m0, m1, m2, m3 = sums
        return (
            m0 + fold(start * start),
            m1 + fold(start * second),
            m2 + fold(second * second),
            m3 + fold(second * image),
        )

    lhs_p = jnp.concatenate(
        [jnp.concatenate([byt[0], byt[0]], axis=1), jnp.concatenate([byt[1], byt[1]], axis=1)], axis=0
    )
    fields = ((xe, 3), (u0, 2), (u1, 1))

    def put_proj(x):
        p = pe[x + 1]
        upper = jnp.where(jnp.logical_and(last, x == LX - 1), 1.0, 0.5)
        lower = jnp.where(jnp.logical_and(first, x == 0), 1.0, 0.5)
        p_rim = rim * p
        p_up = upper * (pe[x + 2] - p)
        p_down = lower * (p - pe[x])
        p_y = inner_y * (pltpu.roll(p, NG - 1, 0) - p)
        p_z = inner_z * (pltpu.roll(p, NG - 1, 1) - p)
        k = kp[x + HALO]
        parts = []
        for ref, at in fields:
            a = ref[x + at]
            total = p_rim * a + (ref[x + at + 1] - a) * p_up + (a - ref[x + at - 1]) * p_down
            qy = (pltpu.roll(a, NG - 1, 0) - a) * p_y
            total = total + (qy + pltpu.roll(qy, 1, 0))
            qz = (pltpu.roll(a, NG - 1, 1) - a) * p_z
            total = total + (qz + pltpu.roll(qz, 1, 1))
            parts.append(jnp.concatenate(pieces(k * total, 2), axis=0))
        got = mm(lhs_p, jnp.concatenate(parts, axis=1))
        got = got[:M] + got[M:]
        for f in range(3):
            pbuf[f, x] = got[:, f * NG : (f + 1) * NG]

    def mix_x(layers, fresh):
        def one(i, carry):
            for f in range(3):
                total = None if fresh else qbuf[f, i]
                for x in layers:
                    term = bx_ref[i, s * LX + x] * pbuf[f, x]
                    total = term if total is None else total + term
                qbuf[f, i] = total
            return carry

        lax.fori_loop(0, M, one, 0)

    def outer(t, count, width):
        return t + jnp.where(t >= width, count - 2 * width, 0)

    load_x.wait()
    lax.fori_loop(3, 17, lambda e, c: (put_u0(e), c)[1], 0)
    lax.fori_loop(3, 15, lambda e, c: (put_u1(e), c)[1], 0)
    zero = jnp.zeros((8, NG), F32)
    sums = lax.fori_loop(3, 13, moments, (zero, zero, zero, zero))
    lax.fori_loop(3, 13, lambda x, c: (put_proj(x), c)[1], 0)
    mix_x(range(3, 13), True)

    load_c.wait()
    pltpu.make_async_copy(cs.at[pl.ds(1, NP - 1)], cs.at[pl.ds(1, NP - 1)], c_recv).wait()
    every = cs[...]
    mine = cs[0]
    gap = every - mine[None]
    near = jnp.sum(jnp.sum(gap * gap, axis=1), axis=1, keepdims=True)
    center = jnp.sum(every, axis=0) * (1.0 / NP)
    off = every - center[None]
    spread = jnp.sum(jnp.sum(off * off, axis=0), keepdims=True) * (2.0 / (NP - 1))
    lane32 = lax.broadcasted_iota(jnp.int32, (NP, NG), 1)
    diag = lane32 == lax.broadcasted_iota(jnp.int32, (NP, NG), 0)
    near_row = jnp.sum(jnp.where(diag, near, 0.0), axis=0, keepdims=True)
    near_row = jnp.where(lane32[0:1] == NP, spread, near_row)
    tail = jnp.concatenate([jnp.broadcast_to(tau, (1, NG)), near_row, jnp.zeros((6, NG), F32)], axis=0)

    @pl.when(jnp.logical_not(first))
    def _():
        x_up().wait_recv()
        r_up().wait_recv()

    @pl.when(jnp.logical_not(last))
    def _():
        x_down().wait_recv()
        r_down().wait_recv()

    lax.fori_loop(0, 6, lambda t, c: (put_u0(outer(t, LX + 4, 3)), c)[1], 0)
    lax.fori_loop(0, 6, lambda t, c: (put_u1(outer(t, LX + 2, 3)), c)[1], 0)
    sums = lax.fori_loop(0, 6, lambda t, c: moments(outer(t, LX, 3), c), sums)

    @pl.when(jnp.logical_not(first))
    def _():
        p_up().wait_recv()

    @pl.when(jnp.logical_not(last))
    def _():
        p_down().wait_recv()

    lax.fori_loop(0, 6, lambda t, c: (put_proj(outer(t, LX, 3)), c)[1], 0)
    mix_x((0, 1, 2, 13, 14, 15), False)

    q_two = jnp.concatenate(pieces(qbuf[...].reshape(3 * M * M, NG), 2), axis=1)
    lhs_z = jnp.concatenate(
        [jnp.concatenate([bzt[0], bzt[0]], axis=1), jnp.concatenate([bzt[1], bzt[1]], axis=1)], axis=0
    )
    tensor = mm_nt(lhs_z, q_two)
    tensor = tensor[:M] + tensor[M:]
    parts = []
    for f in range(3):
        parts += pieces(tensor[:, f * M * M : (f + 1) * M * M], 2)
    rhs = jnp.concatenate(parts, axis=0)

    m3 = sums[3] * tau
    rows = [jnp.sum(m, axis=0, keepdims=True) for m in (sums[0], sums[1], sums[2], m3)]
    head = jnp.concatenate(rows, axis=0)

    def fill(ref, r):
        share = lax.rem(s + r, NS)
        cols = pl.ds(pl.multiple_of(share * SH, SH), SH)
        got = mm(rhs, hot[:, cols])
        low = lhot[:, cols]
        for f in range(3):
            at = 2 * M * f
            row = jnp.sum((got[at : at + M] + got[at + M : at + 2 * M]) * low, axis=0, keepdims=True)
            for q in range(SH // NG):
                ref[r, 4 * f + q : 4 * f + q + 1, :] = row[:, q * NG : (q + 1) * NG]
        ref[r, 12:16, :] = head
        ref[r, 16:24, :] = tail

    def share_send(r, carry):
        fill(pk, r)
        remote(pk.at[r], rp.at[NS - r], r_send, r_recv, peer_s(r)).start()
        return carry

    lax.fori_loop(1, NS, share_send, 0)
    fill(rp, 0)
    pltpu.make_async_copy(rp.at[pl.ds(1, NS - 1)], rp.at[pl.ds(1, NS - 1)], r_recv).wait()

    taus = rp[:, 16:17, :]
    least = jnp.min(taus, axis=0)
    ratio = least[None] / taus
    q0 = jnp.sum(jnp.sum(rp[:, 12:13, :], axis=0), axis=1, keepdims=True)
    q1 = jnp.sum(jnp.sum(rp[:, 13:14, :] * ratio, axis=0), axis=1, keepdims=True)
    q2 = jnp.sum(jnp.sum(rp[:, 14:15, :] * ratio * ratio, axis=0), axis=1, keepdims=True)
    q3 = jnp.sum(jnp.sum(rp[:, 15:16, :] * ratio * ratio * ratio, axis=0), axis=1, keepdims=True)
    proj0 = jnp.sum(rp[:, 0:4, :], axis=0)
    proj1 = jnp.sum(rp[:, 4:8, :], axis=0)
    proj2 = jnp.sum(rp[:, 8:12, :] * ratio, axis=0)
    alpha = q0 / q1
    norm = alpha * alpha * q2 - q0
    grown = norm / q0 + 1.0
    alpha1 = norm / (alpha * alpha * (q3 - q2 * (q2 / q1)))
    tau0 = least[:, 0:1]
    scale0 = tau0 * (alpha + alpha1 * grown)
    scale2 = -(tau0 * alpha1) * alpha
    gs[0] = proj0 + scale0 * proj1 + scale2 * proj2

    def send_g(r, carry):
        remote(gs.at[0], gs.at[NP - r], g_send, g_recv, peer_p(r)).start()
        return carry

    lax.fori_loop(1, NP, send_g, 0)

    scale1 = scale2 * (tau0 / tau)

    def put_x(x, carry):
        xo[x] = xe[x + 3] + scale0 * u0[x + 2] + scale1 * u1[x + 1]
        return carry

    lax.fori_loop(0, LX, put_x, 0)
    store = pltpu.make_async_copy(xo, adj_hbm, out_sem)
    store.start()

    near_all = jnp.sum(rp[:, 17:18, :], axis=0)
    width = near_all[:, NP : NP + 1]
    kern = jnp.exp(-near_all / width)
    kcol = jnp.sum(jnp.where(diag, kern, 0.0), axis=1, keepdims=True)
    weight = jnp.broadcast_to(kcol[:, :, None], (NP, 1, NG))
    drive = jnp.sum(weight * every, axis=0)
    repel = jnp.sum(weight * (mine[None] - every), axis=0)
    base = mine + (STEP / NP) * ((2.0 / width) * repel - drive)

    pltpu.make_async_copy(gs.at[pl.ds(1, NP - 1)], gs.at[pl.ds(1, NP - 1)], g_recv).wait()
    new_ref[...] = base - (STEP / NP) * jnp.sum(weight * gs[...], axis=0)

    def sent(ref, sem):
        pltpu.make_async_copy(ref, ref, sem).wait()

    sent(cs.at[pl.ds(1, NP - 1)], c_send)
    sent(rp.at[pl.ds(1, NS - 1)], r_send)
    sent(gs.at[pl.ds(1, NP - 1)], g_send)

    @pl.when(jnp.logical_not(last))
    def _():
        x_up().wait_send()
        p_up().wait_send()
        r_up().wait_send()

    @pl.when(jnp.logical_not(first))
    def _():
        x_down().wait_send()
        p_down().wait_send()
        r_down().wait_send()

    store.wait()


def shards(coeffs, modes, basis_x, basis_y, basis_z, pressure, initial_adjoint, sensors, observed, precision):
    vmem = pl.BlockSpec(memory_space=pltpu.VMEM)
    smem = pl.BlockSpec(memory_space=pltpu.SMEM)
    anywhere = pl.BlockSpec(memory_space=pl.ANY)
    dma = pltpu.SemaphoreType.DMA
    layers = lambda count: pltpu.VMEM((count, NG, NG), F32)
    new, adjoint = pl.pallas_call(
        kernel,
        out_shape=(
            jax.ShapeDtypeStruct((SH // NG, NG), F32),
            jax.ShapeDtypeStruct((LX, NG, NG), F32),
        ),
        in_specs=[anywhere, vmem, smem, vmem, vmem, anywhere, anywhere, smem, smem, smem],
        out_specs=(vmem, anywhere),
        scratch_shapes=[
            layers(LX + 6),
            layers(LX + 2),
            layers(LX + 6),
            layers(LX + 6),
            layers(LX + 6),
            layers(LX + 6),
            layers(LX + 6),
            layers(LX + 4),
            layers(LX + 2),
            layers(LX),
            pltpu.VMEM((LX + 4, 8, NG), F32),
            pltpu.VMEM((M * M, K), BF16),
            pltpu.VMEM((M, K), F32),
            pltpu.VMEM((3 * M, K), BF16),
            pltpu.VMEM((M, M, NG), F32),
            pltpu.VMEM((3, LX, M, NG), F32),
            pltpu.VMEM((3, M, M, NG), F32),
            pltpu.VMEM((NP, SH // NG, NG), F32),
            pltpu.VMEM((NS, SH // NG, NG), F32),
            pltpu.VMEM((NS, 24, NG), F32),
            pltpu.VMEM((NS, 24, NG), F32),
            pltpu.VMEM((NP, SH // NG, NG), F32),
            dma((3,)), dma, dma((6,)), dma((6,)),
            dma, dma, dma, dma, dma, dma, dma,
        ],
        compiler_params=pltpu.CompilerParams(
            collective_id=0, has_side_effects=True, vmem_limit_bytes=60 * 2**20
        ),
    )(
        coeffs.reshape(NS, SH // NG, NG),
        modes.reshape(K // NG, NG),
        basis_x.T,
        basis_y.T,
        basis_z.T,
        pressure[0],
        initial_adjoint[0],
        sensors,
        observed,
        precision,
    )
    return new.reshape(1, SH), adjoint[None]


def solution(mesh):
    in_specs = (
        P("particle", None),
        P(),
        P(),
        P(),
        P(),
        P("particle", "space", None, None),
        P("particle", "space", None, None),
        P(),
        P(),
        P(),
    )
    out_specs = (P("particle", "space"), P("particle", "space", None, None))
    return jax.shard_map(shards, mesh=mesh, in_specs=in_specs, out_specs=out_specs, check_vma=False)
```

time: 50.1 us -> 47.5 us (0.948)
  Pallas kernels: 45.7 us -> 43.1 us
    pallas_call x1, Pallas kernels: 45.7 us -> 43.1 us  [shards(): pl.pallas_call(kernel, out_shape=(jax.ShapeDtypeStruct((SH // NG, NG), F3...]
where the time goes in v3:
time: 47.5 us; the launch traced here: 47.3 us
  Pallas kernels  43.1 us (91%)
  local copies, waits for them, and re-layouts  3.52 us (7%)
  between operations  0.65 us (1%)
    pallas_call x1, Pallas kernels, shards(): pl.pallas_call(kernel, out_shape=(jax.ShapeDtypeStruct((SH // NG, NG), F3...  43.1 us
    unnamed x4, local copies, waits for them, and re-layouts  3.52 us

profile of v3, /device:TPU:1, one launch (start us, length us, event | category | flops | bytes accessed | tf_op | source)
XLA Modules:
  0.0 47.3 jit_solution(1455043474480468275)
XLA Ops:
  0.6 43.1 %shard_map.113 = (f32[4,128]{1,0:T(4,128)}, f32[16,128,128]{2,1,0:T(8,128)}) custom-call(f32[8,4,128]{2,1,0:T(4,128)} %bitcast.12, s32[32,128]{1,0:T(8,128)} %bitcast.13, f32[16,128]{1,0:T(8,128)} %bitcast.14, f32[16,128]{1,0:T(8,128)} %bitcast.15, f32[16,128]{1,0:T(8,128)} %bitcast.16, f32[16,128,128]{2,1,0:T(8,128)} %bitcast.9, f32[16,128,128]{2,1,0:T(8,128)} %bitcast.10, ...), custom_call_target="tpu_custom_call" | custom-call | tf_op jit(solution)/shard_map/pallas_call | solution.py:481
  43.7 0.0 copy-start
  43.8 0.6 %copy-done = f32[4,128]{1,0:T(4,128)S(1)} copy-done((f32[4,128]{1,0:T(4,128)S(1)}, f32[4,128]{1,0:T(4,128)}, u32[]{:S(2)}) %copy-start) | copy-done | bytes 2072
  44.4 0.6 %copy.14 = f32[1,512]{1,0:T(1,128)} copy(f32[1,512]{1,0:T(1,128)S(1)} %bitcast.17) | data formatting | bytes 4096
  45.0 2.3 %copy.15 = f32[1,16,128,128]{3,2,1,0:T(8,128)} copy(f32[1,16,128,128]{3,2,1,0:T(8,128)} %bitcast.11) | data formatting | bytes 2097152
Async XLA Ops:
  43.7 0.7 %copy-start = (f32[4,128]{1,0:T(4,128)S(1)}, f32[4,128]{1,0:T(4,128)}, u32[]{:S(2)}) copy-start(f32[4,128]{1,0:T(4,128)} %get-tuple-element.4) | copy-start | bytes 6148

commit v4 on v3

--- a/solution.py
+++ b/solution.py
@@ -44,16 +44,20 @@
 
 def kernel(
     c_hbm, modes_ref, bx_ref, by_ref, bz_ref, p_hbm, x_hbm, sens_ref, obs_ref, prec_ref,
-    new_ref, adj_hbm,
-    xe, pe, kp, kx, ky, kz, kb, u0, u1, xo, rsum, hot, lhot, lcs, fbuf, pbuf, qbuf,
+    new_ref, adj_ref,
+    xe, pe, kp, kx, ky, kz, kb, wf, u0, u1, rsum, hot, lhot, lcs, fbuf, pbuf, qbuf,
     cs, wk, pk, rp, gs,
-    in_sem, out_sem, halo_send, halo_recv, c_own, c_send, c_recv, r_send, r_recv, g_send, g_recv,
+    in_sem, halo_send, halo_recv, c_own, c_send, c_recv, r_send, r_recv, g_send, g_recv,
 ):
     n = lax.axis_index("particle")
     s = lax.axis_index("space")
     first = s == 0
     last = s == NS - 1
 
+    def far(j, count):
+        half = (j + 1) // 2
+        return count // 2 + jnp.where(lax.rem(j, 2) == 0, -half, half)
+
     def peer_p(r):
         return {"particle": lax.rem(n + r, NP)}
 
@@ -66,12 +70,12 @@
         pl.semaphore_signal(barrier, inc=1, device_id=peer_s(r))
         return carry
 
-    def greet_p(r, carry):
-        pl.semaphore_signal(barrier, inc=1, device_id=peer_p(r))
+    def greet_p(j, carry):
+        pl.semaphore_signal(barrier, inc=1, device_id=peer_p(far(j, NP)))
         return carry
 
+    lax.fori_loop(0, NP - 1, greet_p, 0)
     lax.fori_loop(1, NS, greet_s, 0)
-    lax.fori_loop(1, NP, greet_p, 0)
 
     load_x = pltpu.make_async_copy(x_hbm, xe.at[pl.ds(HALO, LX)], in_sem.at[0])
     load_p = pltpu.make_async_copy(p_hbm, pe.at[pl.ds(1, LX)], in_sem.at[1])
@@ -112,6 +116,8 @@
 
     inner_y = jnp.where(suby == NG - 1, 0.0, 0.5)
     inner_z = jnp.where(lane == NG - 1, 0.0, 0.5)
+    inner_ym = jnp.where(suby == 0, 0.0, 0.5)
+    inner_zm = jnp.where(lane == 0, 0.0, 0.5)
     rim = (
         jnp.where(suby == NG - 1, 1.0, 0.0)
         + jnp.where(suby == 0, 1.0, 0.0)
@@ -129,8 +135,10 @@
 
     def faces(e, k, before):
         kp[e] = k
-        ky[e] = inner_y * (k + pltpu.roll(k, NG - 1, 0))
-        kz[e] = inner_z * (k + pltpu.roll(k, NG - 1, 1))
+        ky[0, e] = inner_y * (k + pltpu.roll(k, NG - 1, 0))
+        kz[0, e] = inner_z * (k + pltpu.roll(k, NG - 1, 1))
+        ky[1, e] = inner_ym * (k + pltpu.roll(k, 1, 0))
+        kz[1, e] = inner_zm * (k + pltpu.roll(k, 1, 1))
         kb[e] = rim * k
         kx[before] = 0.5 * (kp[before] + k)
 
@@ -138,11 +146,13 @@
         e = 2 * t
         both = jnp.exp(mm(lhs_y, jnp.concatenate([mix(e), mix(e + 1)], axis=1)))
         k0, k1 = both[:, :NG], both[:, NG:]
-        faces(e, k0, jnp.maximum(e - 1, 0))
+        faces(e, k0, max(e - 1, 0))
         faces(e + 1, k1, e)
         return jnp.maximum(top, jnp.max(jnp.maximum(k0, k1).reshape(NG // 8, 8, NG), axis=0))
 
-    top = lax.fori_loop(0, HALO + LX // 2, log_layers, jnp.zeros((8, NG), F32))
+    top = jnp.zeros((8, NG), F32)
+    for t in range(HALO + LX // 2):
+        top = log_layers(t, top)
     tau = (1.0 / 16.0) / jnp.max(top, keepdims=True)
 
     @pl.when(first)
@@ -233,97 +243,125 @@
 
     lax.fori_loop(1, NP, send_c, 0)
 
-    def apply(v_ref, i, e):
+    def differences(v_ref, i):
         v = v_ref[i]
-        total = kb[e] * v
-        total = total - kx[e] * (v_ref[i + 1] - v)
-        total = total + kx[e - 1] * (v - v_ref[i - 1])
-        fy = ky[e] * (pltpu.roll(v, NG - 1, 0) - v)
-        total = total - (fy - pltpu.roll(fy, 1, 0))
-        fz = kz[e] * (pltpu.roll(v, NG - 1, 1) - v)
-        total = total - (fz - pltpu.roll(fz, 1, 1))
-        return v, total
-
-    def inside(g):
-        return jnp.where(jnp.logical_and(g >= 0, g < NX), 1, 0)
-
-    def put_u0(e):
-        g = s * LX - 2 + e
+        return (
+            v - v_ref[i + 1],
+            v - v_ref[i - 1],
+            v - pltpu.roll(v, NG - 1, 0),
+            v - pltpu.roll(v, 1, 0),
+            v - pltpu.roll(v, NG - 1, 1),
+            v - pltpu.roll(v, 1, 1),
+            v,
+        )
+
+    def weigh(weights, parts):
+        total = weights[0] * parts[0]
+        for weight, part in zip(weights[1:], parts[1:]):
+            total = total + weight * part
+        return total
+
+    def operator(d, e):
+        return weigh((kx[e], kx[e - 1], ky[0, e], ky[1, e], kz[0, e], kz[1, e], kb[e]), d)
+
+    def put_weights(x):
+        k = kp[x + HALO]
+        p = pe[x + 1]
+        upper = jnp.where(jnp.logical_and(last, x == LX - 1), 1.0, 0.5)
+        lower = jnp.where(jnp.logical_and(first, x == 0), 1.0, 0.5)
+        wf[0, x] = (upper * k) * (p - pe[x + 2])
+        wf[1, x] = (lower * k) * (p - pe[x])
+        wf[2, x] = (inner_y * k) * (p - pltpu.roll(p, NG - 1, 0))
+        wf[3, x] = (inner_ym * k) * (p - pltpu.roll(p, 1, 0))
+        wf[4, x] = (inner_z * k) * (p - pltpu.roll(p, NG - 1, 1))
+        wf[5, x] = (inner_zm * k) * (p - pltpu.roll(p, 1, 1))
+        wf[6, x] = kb[x + HALO] * p
+
+    lhs_p = jnp.concatenate(
+        [jnp.concatenate([byt[0], byt[0]], axis=1), jnp.concatenate([byt[1], byt[1]], axis=1)], axis=0
+    )
+
+    def put_proj(f, layers, ds):
+        parts = []
+        for x, d in zip(layers, ds):
+            grad = weigh(tuple(wf[j, x] for j in range(7)), d)
+            parts.append(jnp.concatenate(pieces(grad, 2), axis=0))
+        got = mm(lhs_p, jnp.concatenate(parts, axis=1))
+        got = got[:M] + got[M:]
+        for j, x in enumerate(layers):
+            pbuf[f, x] = got[:, j * NG : (j + 1) * NG]
+
+    def put_u0(x, d):
+        g = s * LX + x
         safe = jnp.clip(g, 0, NX - 1)
-        _, image = apply(xe, e + 1, e + 1)
         load = []
         for b in range(8):
             _, cell = sensor_of(safe, b)
-            load.append(jnp.where(flat == cell, rsum[e, b : b + 1, :], 0.0))
-        value = jnp.concatenate(load, axis=0) - image
-        u0[e] = jnp.where(inside(g) == 1, value, 0.0)
-
-    def put_u1(e):
-        g = s * LX - 1 + e
-        _, image = apply(u0, e + 1, e + 2)
-        u1[e] = jnp.where(inside(g) == 1, image * tau, 0.0)
-
-    def moments(x, sums):
-        second, image = apply(u1, x + 1, x + 3)
-        start = u0[x + 2]
+            load.append(jnp.where(flat == cell, rsum[x + 2, b : b + 1, :], 0.0))
+        u0[x + 2] = jnp.concatenate(load, axis=0) - operator(d, x + HALO)
+
+    def put_u1(x, d):
+        u1[x + 1] = operator(d, x + HALO) * tau
+
+    def step_x(layers, project):
+        ds = [differences(xe, x + 3) for x in layers]
+        for x, d in zip(layers, ds):
+            put_u0(x, d)
+        if project:
+            put_proj(0, layers, ds)
+
+    def step_u0(layers, project):
+        ds = [differences(u0, x + 2) for x in layers]
+        for x, d in zip(layers, ds):
+            put_u1(x, d)
+        if project:
+            put_proj(1, layers, ds)
+
+    def step_u1(layers, sums):
+        ds = [differences(u1, x + 1) for x in layers]
         m0, m1, m2, m3 = sums
-        return (
-            m0 + fold(start * start),
-            m1 + fold(start * second),
-            m2 + fold(second * second),
-            m3 + fold(second * image),
-        )
-
-    lhs_p = jnp.concatenate(
-        [jnp.concatenate([byt[0], byt[0]], axis=1), jnp.concatenate([byt[1], byt[1]], axis=1)], axis=0
+        for x, d in zip(layers, ds):
+            second, image = d[6], operator(d, x + HALO)
+            start = u0[x + 2]
+            m0 = m0 + fold(start * start)
+            m1 = m1 + fold(start * second)
+            m2 = m2 + fold(second * second)
+            m3 = m3 + fold(second * image)
+        put_proj(2, layers, ds)
+        return m0, m1, m2, m3
+
+    def mix_x(layers, fresh):
+        def some(j, carry):
+            for f in range(3):
+                kept = [pbuf[f, x] for x in layers]
+                for i in (4 * j, 4 * j + 1, 4 * j + 2, 4 * j + 3):
+                    total = None if fresh else qbuf[f, i]
+                    for x, part in zip(layers, kept):
+                        term = bx_ref[i, s * LX + x] * part
+                        total = term if total is None else total + term
+                    qbuf[f, i] = total
+            return carry
+
+        lax.fori_loop(0, M // 4, some, 0)
+
+    def pairs(lo, hi, step):
+        def body(j, carry):
+            step((lo + 2 * j, lo + 2 * j + 1))
+            return carry
+
+        lax.fori_loop(0, (hi - lo) // 2, body, 0)
+
+    def around(j):
+        return j, LX - 1 - j
+
+    load_x.wait()
+    pairs(1, LX - 1, lambda layers: [put_weights(x) for x in layers])
+    pairs(1, LX - 1, lambda layers: step_x(layers, True))
+    pairs(2, LX - 2, lambda layers: step_u0(layers, True))
+    zero = jnp.zeros((8, NG), F32)
+    sums = lax.fori_loop(
+        0, LX // 2 - 3, lambda j, c: step_u1((3 + 2 * j, 4 + 2 * j), c), (zero, zero, zero, zero)
     )
-    fields = ((xe, 3), (u0, 2), (u1, 1))
-
-    def put_proj(x):
-        p = pe[x + 1]
-        upper = jnp.where(jnp.logical_and(last, x == LX - 1), 1.0, 0.5)
-        lower = jnp.where(jnp.logical_and(first, x == 0), 1.0, 0.5)
-        p_rim = rim * p
-        p_up = upper * (pe[x + 2] - p)
-        p_down = lower * (p - pe[x])
-        p_y = inner_y * (pltpu.roll(p, NG - 1, 0) - p)
-        p_z = inner_z * (pltpu.roll(p, NG - 1, 1) - p)
-        k = kp[x + HALO]
-        parts = []
-        for ref, at in fields:
-            a = ref[x + at]
-            total = p_rim * a + (ref[x + at + 1] - a) * p_up + (a - ref[x + at - 1]) * p_down
-            qy = (pltpu.roll(a, NG - 1, 0) - a) * p_y
-            total = total + (qy + pltpu.roll(qy, 1, 0))
-            qz = (pltpu.roll(a, NG - 1, 1) - a) * p_z
-            total = total + (qz + pltpu.roll(qz, 1, 1))
-            parts.append(jnp.concatenate(pieces(k * total, 2), axis=0))
-        got = mm(lhs_p, jnp.concatenate(parts, axis=1))
-        got = got[:M] + got[M:]
-        for f in range(3):
-            pbuf[f, x] = got[:, f * NG : (f + 1) * NG]
-
-    def mix_x(layers, fresh):
-        def one(i, carry):
-            for f in range(3):
-                total = None if fresh else qbuf[f, i]
-                for x in layers:
-                    term = bx_ref[i, s * LX + x] * pbuf[f, x]
-                    total = term if total is None else total + term
-                qbuf[f, i] = total
-            return carry
-
-        lax.fori_loop(0, M, one, 0)
-
-    def outer(t, count, width):
-        return t + jnp.where(t >= width, count - 2 * width, 0)
-
-    load_x.wait()
-    lax.fori_loop(3, 17, lambda e, c: (put_u0(e), c)[1], 0)
-    lax.fori_loop(3, 15, lambda e, c: (put_u1(e), c)[1], 0)
-    zero = jnp.zeros((8, NG), F32)
-    sums = lax.fori_loop(3, 13, moments, (zero, zero, zero, zero))
-    lax.fori_loop(3, 13, lambda x, c: (put_proj(x), c)[1], 0)
     mix_x(range(3, 13), True)
 
     load_c.wait()
@@ -351,10 +389,6 @@
         x_down().wait_recv()
         r_down().wait_recv()
 
-    lax.fori_loop(0, 6, lambda t, c: (put_u0(outer(t, LX + 4, 3)), c)[1], 0)
-    lax.fori_loop(0, 6, lambda t, c: (put_u1(outer(t, LX + 2, 3)), c)[1], 0)
-    sums = lax.fori_loop(0, 6, lambda t, c: moments(outer(t, LX, 3), c), sums)
-
     @pl.when(jnp.logical_not(first))
     def _():
         p_up().wait_recv()
@@ -363,7 +397,34 @@
     def _():
         p_down().wait_recv()
 
-    lax.fori_loop(0, 6, lambda t, c: (put_proj(outer(t, LX, 3)), c)[1], 0)
+    for x in around(0):
+        put_weights(x)
+    step_x(around(-2), False)
+    step_x(around(-1), False)
+    step_x(around(0), True)
+
+    @pl.when(first)
+    def _():
+        u0[0:2] = jnp.zeros((2, NG, NG), F32)
+
+    @pl.when(last)
+    def _():
+        u0[LX + 2 :] = jnp.zeros((2, NG, NG), F32)
+
+    step_u0(around(-1), False)
+    step_u0(around(0), True)
+    step_u0(around(1), True)
+
+    @pl.when(first)
+    def _():
+        u1[0:1] = jnp.zeros((1, NG, NG), F32)
+
+    @pl.when(last)
+    def _():
+        u1[LX + 1 :] = jnp.zeros((1, NG, NG), F32)
+
+    for j in range(3):
+        sums = step_u1(around(j), sums)
     mix_x((0, 1, 2, 13, 14, 15), False)
 
     q_two = jnp.concatenate(pieces(qbuf[...].reshape(3 * M * M, NG), 2), axis=1)
@@ -378,38 +439,40 @@
     rhs = jnp.concatenate(parts, axis=0)
 
     m3 = sums[3] * tau
-    rows = [jnp.sum(m, axis=0, keepdims=True) for m in (sums[0], sums[1], sums[2], m3)]
+    rows = [
+        jnp.broadcast_to(jnp.sum(jnp.sum(m, axis=0, keepdims=True), axis=1, keepdims=True), (1, NG))
+        for m in (sums[0], sums[1], sums[2], m3)
+    ]
     head = jnp.concatenate(rows, axis=0)
 
-    def fill(ref, r):
-        share = lax.rem(s + r, NS)
-        cols = pl.ds(pl.multiple_of(share * SH, SH), SH)
+    for share in range(NS):
+        cols = slice(share * SH, (share + 1) * SH)
         got = mm(rhs, hot[:, cols])
         low = lhot[:, cols]
         for f in range(3):
             at = 2 * M * f
             row = jnp.sum((got[at : at + M] + got[at + M : at + 2 * M]) * low, axis=0, keepdims=True)
             for q in range(SH // NG):
-                ref[r, 4 * f + q : 4 * f + q + 1, :] = row[:, q * NG : (q + 1) * NG]
-        ref[r, 12:16, :] = head
-        ref[r, 16:24, :] = tail
-
-    def share_send(r, carry):
-        fill(pk, r)
-        remote(pk.at[r], rp.at[NS - r], r_send, r_recv, peer_s(r)).start()
+                pk[share, 4 * f + q : 4 * f + q + 1, :] = row[:, q * NG : (q + 1) * NG]
+        pk[share, 12:16, :] = head
+        pk[share, 16:24, :] = tail
+
+    def share_send(j, carry):
+        r = far(j, NS)
+        remote(pk.at[lax.rem(s + r, NS)], rp.at[NS - r], r_send, r_recv, peer_s(r)).start()
         return carry
 
-    lax.fori_loop(1, NS, share_send, 0)
-    fill(rp, 0)
+    lax.fori_loop(0, NS - 1, share_send, 0)
+    rp[0] = pk[s]
     pltpu.make_async_copy(rp.at[pl.ds(1, NS - 1)], rp.at[pl.ds(1, NS - 1)], r_recv).wait()
 
     taus = rp[:, 16:17, :]
     least = jnp.min(taus, axis=0)
     ratio = least[None] / taus
-    q0 = jnp.sum(jnp.sum(rp[:, 12:13, :], axis=0), axis=1, keepdims=True)
-    q1 = jnp.sum(jnp.sum(rp[:, 13:14, :] * ratio, axis=0), axis=1, keepdims=True)
-    q2 = jnp.sum(jnp.sum(rp[:, 14:15, :] * ratio * ratio, axis=0), axis=1, keepdims=True)
-    q3 = jnp.sum(jnp.sum(rp[:, 15:16, :] * ratio * ratio * ratio, axis=0), axis=1, keepdims=True)
+    q0 = jnp.sum(rp[:, 12:13, :], axis=0)
+    q1 = jnp.sum(rp[:, 13:14, :] * ratio, axis=0)
+    q2 = jnp.sum(rp[:, 14:15, :] * (ratio * ratio), axis=0)
+    q3 = jnp.sum(rp[:, 15:16, :] * (ratio * ratio * ratio), axis=0)
     proj0 = jnp.sum(rp[:, 0:4, :], axis=0)
     proj1 = jnp.sum(rp[:, 4:8, :], axis=0)
     proj2 = jnp.sum(rp[:, 8:12, :] * ratio, axis=0)
@@ -417,26 +480,25 @@
     norm = alpha * alpha * q2 - q0
     grown = norm / q0 + 1.0
     alpha1 = norm / (alpha * alpha * (q3 - q2 * (q2 / q1)))
-    tau0 = least[:, 0:1]
+    tau0 = least
     scale0 = tau0 * (alpha + alpha1 * grown)
     scale2 = -(tau0 * alpha1) * alpha
     gs[0] = proj0 + scale0 * proj1 + scale2 * proj2
 
-    def send_g(r, carry):
+    def send_g(j, carry):
+        r = far(j, NP)
         remote(gs.at[0], gs.at[NP - r], g_send, g_recv, peer_p(r)).start()
         return carry
 
-    lax.fori_loop(1, NP, send_g, 0)
+    lax.fori_loop(0, NP - 1, send_g, 0)
 
     scale1 = scale2 * (tau0 / tau)
 
     def put_x(x, carry):
-        xo[x] = xe[x + 3] + scale0 * u0[x + 2] + scale1 * u1[x + 1]
+        adj_ref[x] = xe[x + 3] + scale0 * u0[x + 2] + scale1 * u1[x + 1]
         return carry
 
     lax.fori_loop(0, LX, put_x, 0)
-    store = pltpu.make_async_copy(xo, adj_hbm, out_sem)
-    store.start()
 
     near_all = jnp.sum(rp[:, 17:18, :], axis=0)
     width = near_all[:, NP : NP + 1]
@@ -469,34 +531,32 @@
         p_down().wait_send()
         r_down().wait_send()
 
-    store.wait()
-
 
 def shards(coeffs, modes, basis_x, basis_y, basis_z, pressure, initial_adjoint, sensors, observed, precision):
     vmem = pl.BlockSpec(memory_space=pltpu.VMEM)
     smem = pl.BlockSpec(memory_space=pltpu.SMEM)
-    anywhere = pl.BlockSpec(memory_space=pl.ANY)
+    hbm = pl.BlockSpec(memory_space=pltpu.HBM)
     dma = pltpu.SemaphoreType.DMA
     layers = lambda count: pltpu.VMEM((count, NG, NG), F32)
     new, adjoint = pl.pallas_call(
         kernel,
         out_shape=(
-            jax.ShapeDtypeStruct((SH // NG, NG), F32),
-            jax.ShapeDtypeStruct((LX, NG, NG), F32),
+            pltpu.VMEM((SH // NG, NG), F32),
+            pltpu.VMEM((LX, NG, NG), F32),
         ),
-        in_specs=[anywhere, vmem, smem, vmem, vmem, anywhere, anywhere, smem, smem, smem],
-        out_specs=(vmem, anywhere),
+        in_specs=[hbm, vmem, smem, vmem, vmem, hbm, hbm, smem, smem, smem],
+        out_specs=(vmem, vmem),
         scratch_shapes=[
             layers(LX + 6),
             layers(LX + 2),
             layers(LX + 6),
             layers(LX + 6),
+            pltpu.VMEM((2, LX + 6, NG, NG), F32),
+            pltpu.VMEM((2, LX + 6, NG, NG), F32),
             layers(LX + 6),
-            layers(LX + 6),
-            layers(LX + 6),
+            pltpu.VMEM((7, LX, NG, NG), F32),
             layers(LX + 4),
             layers(LX + 2),
-            layers(LX),
             pltpu.VMEM((LX + 4, 8, NG), F32),
             pltpu.VMEM((M * M, K), BF16),
             pltpu.VMEM((M, K), F32),
@@ -509,7 +569,7 @@
             pltpu.VMEM((NS, 24, NG), F32),
             pltpu.VMEM((NS, 24, NG), F32),
             pltpu.VMEM((NP, SH // NG, NG), F32),
-            dma((3,)), dma, dma((6,)), dma((6,)),
+            dma((3,)), dma((6,)), dma((6,)),
             dma, dma, dma, dma, dma, dma, dma,
         ],
         compiler_params=pltpu.CompilerParams(

time: 47.5 us -> 37.5 us (0.79)
  Pallas kernels: 43.1 us -> 35.2 us
  local copies, waits for them, and re-layouts: 3.52 us -> 1.55 us
    pallas_call x1, Pallas kernels: 43.1 us -> 35.2 us  [shards(): pl.pallas_call(kernel, out_shape=(pltpu.VMEM((SH // NG, NG), F32), pltpu....]
    unnamed x4 -> x2, local copies, waits for them, and re-layouts: 3.52 us -> 1.55 us
where the time goes in v4:
time: 37.5 us; the launch traced here: 37.3 us
  Pallas kernels  35.2 us (94%)
  local copies, waits for them, and re-layouts  1.55 us (4%)
  between operations  0.64 us (2%)
    pallas_call x1, Pallas kernels, shards(): pl.pallas_call(kernel, out_shape=(pltpu.VMEM((SH // NG, NG), F32), pltpu....  35.2 us
    unnamed x2, local copies, waits for them, and re-layouts  1.55 us

profile of v4, /device:TPU:1, one launch (start us, length us, event | category | flops | bytes accessed | tf_op | source)
XLA Modules:
  0.0 37.3 jit_solution(11940256164214336701)
XLA Ops:
  0.6 35.2 %shard_map.113 = (f32[4,128]{1,0:T(4,128)S(1)}, f32[16,128,128]{2,1,0:T(8,128)S(1)}) custom-call(f32[8,4,128]{2,1,0:T(4,128)} %bitcast.13, s32[32,128]{1,0:T(8,128)} %bitcast.14, f32[16,128]{1,0:T(8,128)} %bitcast.15, f32[16,128]{1,0:T(8,128)} %bitcast.16, f32[16,128]{1,0:T(8,128)} %bitcast.17, f32[16,128,128]{2,1,0:T(8,128)} %bitcast.11, ...), custom_call_target="tpu_custom_call" | custom-call | tf_op jit(solution)/shard_map/pallas_call | solution.py:541
  35.8 0.6 %copy.14 = f32[1,512]{1,0:T(1,128)} copy(f32[1,512]{1,0:T(1,128)S(1)} %bitcast.10) | data formatting | bytes 4096
  36.4 1.0 %copy.15 = f32[1,16,128,128]{3,2,1,0:T(8,128)} copy(f32[1,16,128,128]{3,2,1,0:T(8,128)S(1)} %bitcast.9) | data formatting | bytes 2097152

commit v5 on v4

--- a/solution.py
+++ b/solution.py
@@ -43,11 +43,11 @@
 
 
 def kernel(
-    c_hbm, modes_ref, bx_ref, by_ref, bz_ref, p_hbm, x_hbm, sens_ref, obs_ref, prec_ref,
+    c_hbm, modes_in, bx_in, by_in, bz_in, p_hbm, x_hbm, sens_in, obs_in, prec_in,
     new_ref, adj_ref,
-    xe, pe, kp, kx, ky, kz, kb, wf, u0, u1, rsum, hot, lhot, lcs, fbuf, pbuf, qbuf,
+    modes_ref, bx_ref, by_ref, bz_ref, sens_ref, obs_ref, prec_ref, xe, pe, kp, kx, ky, kz, kb, wf, u0, u1, rsum, hot, lhot, lcs, fbuf, pbuf, qbuf,
     cs, wk, pk, rp, gs,
-    in_sem, halo_send, halo_recv, c_own, c_send, c_recv, r_send, r_recv, g_send, g_recv,
+    in_sem, small_sem, halo_send, halo_recv, c_own, c_send, c_recv, r_send, r_recv, g_send, g_recv,
 ):
     n = lax.axis_index("particle")
     s = lax.axis_index("space")
@@ -56,7 +56,7 @@
 
     def far(j, count):
         half = (j + 1) // 2
-        return count // 2 + jnp.where(lax.rem(j, 2) == 0, -half, half)
+        return count // 2 + (half if j % 2 else -half)
 
     def peer_p(r):
         return {"particle": lax.rem(n + r, NP)}
@@ -65,28 +65,32 @@
         return {"space": lax.rem(s + r, NS)}
 
     barrier = pltpu.get_barrier_semaphore()
-
-    def greet_s(r, carry):
-        pl.semaphore_signal(barrier, inc=1, device_id=peer_s(r))
-        return carry
-
-    def greet_p(j, carry):
-        pl.semaphore_signal(barrier, inc=1, device_id=peer_p(far(j, NP)))
-        return carry
-
-    lax.fori_loop(0, NP - 1, greet_p, 0)
-    lax.fori_loop(1, NS, greet_s, 0)
 
     load_x = pltpu.make_async_copy(x_hbm, xe.at[pl.ds(HALO, LX)], in_sem.at[0])
     load_p = pltpu.make_async_copy(p_hbm, pe.at[pl.ds(1, LX)], in_sem.at[1])
     load_c = pltpu.make_async_copy(c_hbm.at[s], cs.at[0], c_own)
     load_all = pltpu.make_async_copy(c_hbm, wk, in_sem.at[2])
+    small = (
+        (modes_in, modes_ref), (bx_in, bx_ref), (by_in, by_ref), (bz_in, bz_ref),
+        (sens_in, sens_ref), (obs_in, obs_ref), (prec_in, prec_ref),
+    )
+    load_small = [pltpu.make_async_copy(src, dst, small_sem.at[j]) for j, (src, dst) in enumerate(small)]
     load_all.start()
+    load_small[0].start()
+
+    for j in range(NP - 1):
+        pl.semaphore_signal(barrier, inc=1, device_id=peer_p(far(j, NP)))
+    for r in range(1, NS):
+        pl.semaphore_signal(barrier, inc=1, device_id=peer_s(r))
+
+    for load in load_small[1:]:
+        load.start()
     load_p.start()
     load_x.start()
     load_c.start()
 
     load_all.wait()
+    load_small[0].wait()
     row_id = lax.broadcasted_iota(jnp.int32, (M * M, NG), 0)
     sub_id = lax.broadcasted_iota(jnp.int32, (M, NG), 0)
     for chunk in range(K // NG):
@@ -104,6 +108,8 @@
     lane = lax.broadcasted_iota(jnp.int32, (NG, NG), 1)
     suby = lax.broadcasted_iota(jnp.int32, (NG, NG), 0)
     eye = jnp.where(lane == suby, 1.0, 0.0).astype(BF16)
+    for load in load_small[1:4]:
+        load.wait()
     byt = pieces(by_ref[...], 3)
     bzt = pieces(bz_ref[...], 3)
     lhs_y = mm_nt(eye, jnp.concatenate([byt[which] for which in (0, 0, 1, 0, 1, 2)], axis=0)).astype(BF16)
@@ -176,6 +182,8 @@
         return index, sens_ref[index] - index * (M * NG)
 
     load_p.wait()
+    for load in load_small[4:]:
+        load.wait()
 
     def misfit(x, carry):
         for b in range(8):
@@ -457,12 +465,9 @@
         pk[share, 12:16, :] = head
         pk[share, 16:24, :] = tail
 
-    def share_send(j, carry):
+    for j in range(NS - 1):
         r = far(j, NS)
         remote(pk.at[lax.rem(s + r, NS)], rp.at[NS - r], r_send, r_recv, peer_s(r)).start()
-        return carry
-
-    lax.fori_loop(0, NS - 1, share_send, 0)
     rp[0] = pk[s]
     pltpu.make_async_copy(rp.at[pl.ds(1, NS - 1)], rp.at[pl.ds(1, NS - 1)], r_recv).wait()
 
@@ -485,12 +490,9 @@
     scale2 = -(tau0 * alpha1) * alpha
     gs[0] = proj0 + scale0 * proj1 + scale2 * proj2
 
-    def send_g(j, carry):
+    for j in range(NP - 1):
         r = far(j, NP)
         remote(gs.at[0], gs.at[NP - r], g_send, g_recv, peer_p(r)).start()
-        return carry
-
-    lax.fori_loop(0, NP - 1, send_g, 0)
 
     scale1 = scale2 * (tau0 / tau)
 
@@ -534,7 +536,6 @@
 
 def shards(coeffs, modes, basis_x, basis_y, basis_z, pressure, initial_adjoint, sensors, observed, precision):
     vmem = pl.BlockSpec(memory_space=pltpu.VMEM)
-    smem = pl.BlockSpec(memory_space=pltpu.SMEM)
     hbm = pl.BlockSpec(memory_space=pltpu.HBM)
     dma = pltpu.SemaphoreType.DMA
     layers = lambda count: pltpu.VMEM((count, NG, NG), F32)
@@ -544,9 +545,16 @@
             pltpu.VMEM((SH // NG, NG), F32),
             pltpu.VMEM((LX, NG, NG), F32),
         ),
-        in_specs=[hbm, vmem, smem, vmem, vmem, hbm, hbm, smem, smem, smem],
+        in_specs=[hbm] * 10,
         out_specs=(vmem, vmem),
         scratch_shapes=[
+            pltpu.VMEM((K // NG, NG), jnp.int32),
+            pltpu.SMEM((M, NX), F32),
+            pltpu.VMEM((M, NG), F32),
+            pltpu.VMEM((M, NG), F32),
+            pltpu.SMEM(sensors.shape, jnp.int32),
+            pltpu.SMEM(sensors.shape, F32),
+            pltpu.SMEM(sensors.shape, F32),
             layers(LX + 6),
             layers(LX + 2),
             layers(LX + 6),
@@ -569,7 +577,7 @@
             pltpu.VMEM((NS, 24, NG), F32),
             pltpu.VMEM((NS, 24, NG), F32),
             pltpu.VMEM((NP, SH // NG, NG), F32),
-            dma((3,)), dma((6,)), dma((6,)),
+            dma((3,)), dma((7,)), dma((6,)), dma((6,)),
             dma, dma, dma, dma, dma, dma, dma,
         ],
         compiler_params=pltpu.CompilerParams(

time: 37.5 us -> 36.1 us (0.963)
  Pallas kernels: 35.2 us -> 33.7 us
    pallas_call x1, Pallas kernels: 35.2 us -> 33.7 us  [shards(): pl.pallas_call(kernel, out_shape=(pltpu.VMEM((SH // NG, NG), F32), pltpu....]
where the time goes in v5:
time: 36.1 us; the launch traced here: 35.9 us
  Pallas kernels  33.7 us (93%)
  local copies, waits for them, and re-layouts  1.55 us (4%)
  between operations  0.64 us (2%)
    pallas_call x1, Pallas kernels, shards(): pl.pallas_call(kernel, out_shape=(pltpu.VMEM((SH // NG, NG), F32), pltpu....  33.7 us
    unnamed x2, local copies, waits for them, and re-layouts  1.55 us

profile of v5, /device:TPU:1, one launch (start us, length us, event | category | flops | bytes accessed | tf_op | source)
XLA Modules:
  0.0 35.9 jit_solution(17217406897439278345)
XLA Ops:
  0.6 33.7 %shard_map.113 = (f32[4,128]{1,0:T(4,128)S(1)}, f32[16,128,128]{2,1,0:T(8,128)S(1)}) custom-call(f32[8,4,128]{2,1,0:T(4,128)} %bitcast.13, s32[32,128]{1,0:T(8,128)} %bitcast.14, f32[16,128]{1,0:T(8,128)} %bitcast.15, f32[16,128]{1,0:T(8,128)} %bitcast.16, f32[16,128]{1,0:T(8,128)} %bitcast.17, f32[16,128,128]{2,1,0:T(8,128)} %bitcast.11, ...), custom_call_target="tpu_custom_call" | custom-call | tf_op jit(solution)/shard_map/pallas_call | solution.py:542
  34.4 0.6 %copy.14 = f32[1,512]{1,0:T(1,128)} copy(f32[1,512]{1,0:T(1,128)S(1)} %bitcast.10) | data formatting | bytes 4096
  34.9 1.0 %copy.15 = f32[1,16,128,128]{3,2,1,0:T(8,128)} copy(f32[1,16,128,128]{3,2,1,0:T(8,128)S(1)} %bitcast.9) | data formatting | bytes 2097152

commit v6 on v5

--- a/solution.py
+++ b/solution.py
@@ -173,6 +173,52 @@
         pe[LX + 1 :] = jnp.zeros((1, NG, NG), F32)
         rsum[LX + 2 :] = jnp.zeros((2, 8, NG), F32)
 
+    pl.semaphore_wait(barrier, NS - 1 + NP - 1)
+
+    up = {"space": jnp.minimum(s + 1, NS - 1)}
+    down = {"space": jnp.maximum(s - 1, 0)}
+
+    def remote(src, dst, send, recv, where):
+        return pltpu.make_async_remote_copy(src_ref=src, dst_ref=dst, send_sem=send, recv_sem=recv, device_id=where)
+
+    def x_up():
+        return remote(x_hbm.at[pl.ds(LX - HALO, HALO)], xe.at[pl.ds(0, HALO)], halo_send.at[0], halo_recv.at[0], up)
+
+    def x_down():
+        return remote(x_hbm.at[pl.ds(0, HALO)], xe.at[pl.ds(HALO + LX, HALO)], halo_send.at[1], halo_recv.at[1], down)
+
+    def p_up():
+        return remote(p_hbm.at[pl.ds(LX - 1, 1)], pe.at[pl.ds(0, 1)], halo_send.at[2], halo_recv.at[2], up)
+
+    def p_down():
+        return remote(p_hbm.at[pl.ds(0, 1)], pe.at[pl.ds(LX + 1, 1)], halo_send.at[3], halo_recv.at[3], down)
+
+    def r_up():
+        return remote(rsum.at[pl.ds(LX, 2)], rsum.at[pl.ds(0, 2)], halo_send.at[4], halo_recv.at[4], up)
+
+    def r_down():
+        return remote(rsum.at[pl.ds(2, 2)], rsum.at[pl.ds(LX + 2, 2)], halo_send.at[5], halo_recv.at[5], down)
+
+    @pl.when(jnp.logical_not(last))
+    def _():
+        x_up().start()
+
+    @pl.when(jnp.logical_not(first))
+    def _():
+        x_down().start()
+
+    @pl.when(jnp.logical_not(last))
+    def _():
+        p_up().start()
+
+    @pl.when(jnp.logical_not(first))
+    def _():
+        p_down().start()
+
+    def send_c(r, carry):
+        remote(c_hbm.at[s], cs.at[NP - r], c_send, c_recv, peer_p(r)).start()
+        return carry
+
     flat = (
         lax.broadcasted_iota(jnp.int32, (M, NG), 0) * NG + lax.broadcasted_iota(jnp.int32, (M, NG), 1)
     )
@@ -194,52 +240,6 @@
         return carry
 
     lax.fori_loop(0, LX, misfit, 0)
-
-    pl.semaphore_wait(barrier, NS - 1 + NP - 1)
-
-    up = {"space": jnp.minimum(s + 1, NS - 1)}
-    down = {"space": jnp.maximum(s - 1, 0)}
-
-    def remote(src, dst, send, recv, where):
-        return pltpu.make_async_remote_copy(src_ref=src, dst_ref=dst, send_sem=send, recv_sem=recv, device_id=where)
-
-    def x_up():
-        return remote(x_hbm.at[pl.ds(LX - HALO, HALO)], xe.at[pl.ds(0, HALO)], halo_send.at[0], halo_recv.at[0], up)
-
-    def x_down():
-        return remote(x_hbm.at[pl.ds(0, HALO)], xe.at[pl.ds(HALO + LX, HALO)], halo_send.at[1], halo_recv.at[1], down)
-
-    def p_up():
-        return remote(p_hbm.at[pl.ds(LX - 1, 1)], pe.at[pl.ds(0, 1)], halo_send.at[2], halo_recv.at[2], up)
-
-    def p_down():
-        return remote(p_hbm.at[pl.ds(0, 1)], pe.at[pl.ds(LX + 1, 1)], halo_send.at[3], halo_recv.at[3], down)
-
-    def r_up():
-        return remote(rsum.at[pl.ds(LX, 2)], rsum.at[pl.ds(0, 2)], halo_send.at[4], halo_recv.at[4], up)
-
-    def r_down():
-        return remote(rsum.at[pl.ds(2, 2)], rsum.at[pl.ds(LX + 2, 2)], halo_send.at[5], halo_recv.at[5], down)
-
-    @pl.when(jnp.logical_not(last))
-    def _():
-        x_up().start()
-
-    @pl.when(jnp.logical_not(first))
-    def _():
-        x_down().start()
-
-    @pl.when(jnp.logical_not(last))
-    def _():
-        p_up().start()
-
-    @pl.when(jnp.logical_not(first))
-    def _():
-        p_down().start()
-
-    def send_c(r, carry):
-        remote(c_hbm.at[s], cs.at[NP - r], c_send, c_recv, peer_p(r)).start()
-        return carry
 
     @pl.when(jnp.logical_not(last))
     def _():
@@ -352,12 +352,12 @@
 
         lax.fori_loop(0, M // 4, some, 0)
 
-    def pairs(lo, hi, step):
+    def pairs(lo, hi, step, wide=2):
         def body(j, carry):
-            step((lo + 2 * j, lo + 2 * j + 1))
+            step(tuple(lo + wide * j + i for i in range(wide)))
             return carry
 
-        lax.fori_loop(0, (hi - lo) // 2, body, 0)
+        lax.fori_loop(0, (hi - lo) // wide, body, 0)
 
     def around(j):
         return j, LX - 1 - j
@@ -365,7 +365,7 @@
     load_x.wait()
     pairs(1, LX - 1, lambda layers: [put_weights(x) for x in layers])
     pairs(1, LX - 1, lambda layers: step_x(layers, True))
-    pairs(2, LX - 2, lambda layers: step_u0(layers, True))
+    pairs(2, LX - 2, lambda layers: step_u0(layers, True), 4)
     zero = jnp.zeros((8, NG), F32)
     sums = lax.fori_loop(
         0, LX // 2 - 3, lambda j, c: step_u1((3 + 2 * j, 4 + 2 * j), c), (zero, zero, zero, zero)
@@ -465,9 +465,12 @@
         pk[share, 12:16, :] = head
         pk[share, 16:24, :] = tail
 
-    for j in range(NS - 1):
-        r = far(j, NS)
-        remote(pk.at[lax.rem(s + r, NS)], rp.at[NS - r], r_send, r_recv, peer_s(r)).start()
+        @pl.when(s != share)
+        def _():
+            to = rp.at[lax.rem(s - share + NS, NS)]
+            remote(pk.at[share], to, r_send, r_recv, {"space": share}).start()
+
+
     rp[0] = pk[s]
     pltpu.make_async_copy(rp.at[pl.ds(1, NS - 1)], rp.at[pl.ds(1, NS - 1)], r_recv).wait()
 

time: 36.1 us -> 35.1 us (0.972)
  Pallas kernels: 33.7 us -> 32.7 us
    pallas_call x1, Pallas kernels: 33.7 us -> 32.7 us  [shards(): pl.pallas_call(kernel, out_shape=(pltpu.VMEM((SH // NG, NG), F32), pltpu....]
where the time goes in v6:
time: 35.1 us; the launch traced here: 34.9 us
  Pallas kernels  32.7 us (93%)
  local copies, waits for them, and re-layouts  1.55 us (4%)
  between operations  0.64 us (2%)
    pallas_call x1, Pallas kernels, shards(): pl.pallas_call(kernel, out_shape=(pltpu.VMEM((SH // NG, NG), F32), pltpu....  32.7 us
    unnamed x2, local copies, waits for them, and re-layouts  1.55 us

profile of v6, /device:TPU:1, one launch (start us, length us, event | category | flops | bytes accessed | tf_op | source)
XLA Modules:
  0.0 34.9 jit_solution(12251207157241761786)
XLA Ops:
  0.6 32.7 %shard_map.113 = (f32[4,128]{1,0:T(4,128)S(1)}, f32[16,128,128]{2,1,0:T(8,128)S(1)}) custom-call(f32[8,4,128]{2,1,0:T(4,128)} %bitcast.13, s32[32,128]{1,0:T(8,128)} %bitcast.14, f32[16,128]{1,0:T(8,128)} %bitcast.15, f32[16,128]{1,0:T(8,128)} %bitcast.16, f32[16,128]{1,0:T(8,128)} %bitcast.17, f32[16,128,128]{2,1,0:T(8,128)} %bitcast.11, ...), custom_call_target="tpu_custom_call" | custom-call | tf_op jit(solution)/shard_map/pallas_call | solution.py:545
  33.3 0.6 %copy.14 = f32[1,512]{1,0:T(1,128)} copy(f32[1,512]{1,0:T(1,128)S(1)} %bitcast.10) | data formatting | bytes 4096
  33.9 1.0 %copy.15 = f32[1,16,128,128]{3,2,1,0:T(8,128)} copy(f32[1,16,128,128]{3,2,1,0:T(8,128)S(1)} %bitcast.9) | data formatting | bytes 2097152

commit v7 on v6

--- a/solution.py
+++ b/solution.py
@@ -420,8 +420,7 @@
         u0[LX + 2 :] = jnp.zeros((2, NG, NG), F32)
 
     step_u0(around(-1), False)
-    step_u0(around(0), True)
-    step_u0(around(1), True)
+    step_u0(around(0) + around(1), True)
 
     @pl.when(first)
     def _():
@@ -431,8 +430,7 @@
     def _():
         u1[LX + 1 :] = jnp.zeros((1, NG, NG), F32)
 
-    for j in range(3):
-        sums = step_u1(around(j), sums)
+    sums = step_u1(around(0) + around(1) + around(2), sums)
     mix_x((0, 1, 2, 13, 14, 15), False)
 
     q_two = jnp.concatenate(pieces(qbuf[...].reshape(3 * M * M, NG), 2), axis=1)

time: 35.1 us -> 35.1 us (level)
  no operation moved by 1% of the time
where the time goes in v7:
time: 35.1 us; the launch traced here: 34.9 us
  Pallas kernels  32.7 us (93%)
  local copies, waits for them, and re-layouts  1.55 us (4%)
  between operations  0.64 us (2%)
    pallas_call x1, Pallas kernels, shards(): pl.pallas_call(kernel, out_shape=(pltpu.VMEM((SH // NG, NG), F32), pltpu....  32.7 us
    unnamed x2, local copies, waits for them, and re-layouts  1.55 us

profile of v7, /device:TPU:1, one launch (start us, length us, event | category | flops | bytes accessed | tf_op | source)
XLA Modules:
  0.0 34.9 jit_solution(1058445872722694741)
XLA Ops:
  0.6 32.7 %shard_map.113 = (f32[4,128]{1,0:T(4,128)S(1)}, f32[16,128,128]{2,1,0:T(8,128)S(1)}) custom-call(f32[8,4,128]{2,1,0:T(4,128)} %bitcast.13, s32[32,128]{1,0:T(8,128)} %bitcast.14, f32[16,128]{1,0:T(8,128)} %bitcast.15, f32[16,128]{1,0:T(8,128)} %bitcast.16, f32[16,128]{1,0:T(8,128)} %bitcast.17, f32[16,128,128]{2,1,0:T(8,128)} %bitcast.11, ...), custom_call_target="tpu_custom_call" | custom-call | tf_op jit(solution)/shard_map/pallas_call | solution.py:543
  33.4 0.6 %copy.14 = f32[1,512]{1,0:T(1,128)} copy(f32[1,512]{1,0:T(1,128)S(1)} %bitcast.10) | data formatting | bytes 4096
  33.9 1.0 %copy.15 = f32[1,16,128,128]{3,2,1,0:T(8,128)} copy(f32[1,16,128,128]{3,2,1,0:T(8,128)S(1)} %bitcast.9) | data formatting | bytes 2097152
